TPU v7x, 512 devices: a whole 4x4x16 slice. The times are simulated.
512 devices in a mesh: dp: 32 (over z, core), crow: 4 (over x), ccol: 4 (over y).
Axes of the slice: x: 4, y: 4, z: 16, core: 2. Of those that a mesh axis runs over, the one named last changes fastest.
Arguments:
- data: float32 [16, 262144], P(None, ('dp', 'crow')), may hold values from 0 to 1
- centres: float32 [16, 3072], P(None, 'ccol'), may hold values from 0 to 1
- scales: float32 [16], replicated, may hold values from 0.5 to 1.2
- factor: float32 [3072, 3072], P('crow', 'ccol'), may hold values from -1 to 1, as said below
- block_inv: float32 [12, 256, 256], P('crow'), may hold values from -1 to 2
- iterate: float32 [8, 3072], replicated, may hold values from -6 to 6
- residual: float32 [8, 3072], replicated, may hold values from -6 to 6
- direction: float32 [8, 3072], replicated, may hold values from -6 to 6
Outputs:
- new_iterate: float32 [8, 3072], replicated
- new_residual: float32 [8, 3072], replicated
- new_direction: float32 [8, 3072], replicated
Inputs may be any that keep to these rules, and one draw needn't show every extreme that they name: `factor`: blocks of 256 x 256 on and above the block diagonal are zero.
All inputs are finite; a program needn't handle non-finite values.
Results may differ from a plain program's by a relative error of at most 0.0001.
Values sent between devices are 32-bit elements; how exact they have to be, the bound alone decides.
A program may use at most 64 MiB of HBM per device.

v0:
```python
import jax
import jax.numpy as jnp
from jax import lax
from jax.sharding import PartitionSpec as P

RBLK = 1024


ridge_weight = 0.2
highest = lax.Precision.HIGHEST


def kernel_tile(sample, centre_set, scales):
    scaled_sample = sample / scales[:, None]
    scaled_centres = centre_set / scales[:, None]
    cross_terms = lax.dot_general(
        scaled_centres,
        scaled_sample,
        (((0,), (0,)), ((), ())),
        precision=highest,
        preferred_element_type=jnp.float32,
    )
    distance = (
        jnp.sum(scaled_centres * scaled_centres, axis=0)[:, None]
        + jnp.sum(scaled_sample * scaled_sample, axis=0)[None, :]
        - 2.0 * cross_terms
    )
    return jnp.exp(-0.5 * distance)


def project(weights, tile):
    return jnp.dot(weights, tile, precision=highest, preferred_element_type=jnp.float32)


def pullback(images, tile):
    return lax.dot_general(
        images,
        tile,
        (((1,), (1,)), ((), ())),
        precision=highest,
        preferred_element_type=jnp.float32,
    )


def per_device(data, centres, scales, factor, block_inv, iterate, residual, direction):
    order = block_inv.shape[1]
    local_rows = factor.shape[0]
    local_cols = factor.shape[1]
    per_row = local_rows // order
    per_col = local_cols // order
    nblocks = per_row * lax.axis_size("crow")
    row_place = lax.axis_index("crow")
    col_place = lax.axis_index("ccol")
    solved = jnp.zeros_like(direction)
    for number in reversed(range(nblocks)):
        start = number * order
        owner = number // per_col
        offset = number % per_col * order
        held = number % per_row
        segment = lax.dynamic_slice_in_dim(solved, row_place * local_rows, local_rows, 1)
        partial_value = project(segment, factor[:, offset : offset + order])
        partial_value = jnp.where(col_place == owner, partial_value, 0.0)
        partial_value = lax.psum(partial_value, ("crow", "ccol"))
        piece = project(direction[:, start : start + order] - partial_value, block_inv[held])
        solved = solved.at[:, start : start + order].set(piece)
    own_part = lax.dynamic_slice_in_dim(solved, row_place * local_rows, local_rows, 1)
    solved = lax.all_gather(own_part, "crow", axis=1, tiled=True)
    rows_here = data.shape[1]
    span = min(RBLK, rows_here)
    blocks = rows_here // span
    stacked = data.reshape(data.shape[0], blocks, span).transpose(1, 0, 2)
    width = centres.shape[1]
    mine = lax.dynamic_slice_in_dim(solved, col_place * width, width, 1)

    def forward_images(carry, sample):
        return (carry, project(mine, kernel_tile(sample, centres, scales)))

    _, images = lax.scan(forward_images, jnp.zeros((), jnp.float32), stacked)
    images = lax.psum(images, "ccol")

    def backward_images(total, pair):
        sample, image_rows = pair
        return (total + pullback(image_rows, kernel_tile(sample, centres, scales)), None)

    summed, _ = lax.scan(
        backward_images, jnp.zeros((solved.shape[0], width), jnp.float32), (stacked, images)
    )
    summed = lax.psum(summed, ("dp", "crow"))
    summed = lax.all_gather(summed, "ccol", axis=1, tiled=True)
    total_rows = rows_here * lax.axis_size("dp") * lax.axis_size("crow")
    normal_image = summed / total_rows + ridge_weight * solved
    image = jnp.zeros_like(direction)
    for number in range(nblocks):
        start = number * order
        owner = number // per_row
        held = number % per_row
        offset = held * order
        segment = lax.dynamic_slice_in_dim(image, col_place * local_cols, local_cols, 1)
        leading = jnp.where(col_place == 0, normal_image[:, start : start + order], 0.0)
        term = pullback(
            leading - pullback(segment, factor[offset : offset + order, :]), block_inv[held]
        )
        term = jnp.where(row_place == owner, term, 0.0)
        piece = lax.psum(term, ("crow", "ccol"))
        image = image.at[:, start : start + order].set(piece)
    gamma = jnp.sum(residual * residual, axis=1)
    curvature = jnp.sum(direction * image, axis=1)
    alpha = (gamma / curvature)[:, None]
    new_iterate = iterate + alpha * direction
    new_residual = residual - alpha * image
    gamma_next = jnp.sum(new_residual * new_residual, axis=1)
    new_direction = new_residual + (gamma_next / gamma)[:, None] * direction
    return (new_iterate, new_residual, new_direction)


def solution(mesh):
    placed = (
        P(None, ("dp", "crow")),
        P(None, "ccol"),
        P(),
        P("crow", "ccol"),
        P("crow", None, None),
        P(),
        P(),
        P(),
    )
    return jax.shard_map(
        per_device, mesh=mesh, in_specs=placed, out_specs=(P(), P(), P()), check_vma=False
    )
```

profile of v0, /device:TPU:8, one launch (start us, length us, event | category | flops | bytes accessed | tf_op | source)
XLA Modules:
  0.0 1564.1 jit_solution(2935731484131593567)
XLA Ops:
  14.5 1.5 convolution_select_fusion.34
  16.1 41.8 %psum.182 = f32[8,256]{1,0:T(8,128)S(1)} all-reduce(f32[8,256]{1,0:T(8,128)S(1)} %convolution_select_fusion.34), channel_id=1, replica_groups=mesh['dp'=32,'crow'=4,'ccol'=4] {'crow','ccol'}, use_global_device_ids=true, to_apply=%region_2.3 | all-reduce | flops 2048 | bytes 16384 | tf_op jit(solution)/shard_map/psum | solution.py:63
  57.9 1.2 fusion.98
  59.0 1.6 convolution_select_fusion.33
  60.6 36.0 %psum.183 = f32[8,256]{1,0:T(8,128)S(1)} all-reduce(f32[8,256]{1,0:T(8,128)S(1)} %convolution_select_fusion.33), channel_id=1, replica_groups=mesh['dp'=32,'crow'=4,'ccol'=4] {'crow','ccol'}, use_global_device_ids=true, to_apply=%region_4.5 | all-reduce | flops 2048 | bytes 16384 | tf_op jit(solution)/shard_map/psum | solution.py:63
  96.6 1.8 fusion.50
  98.9 38.1 %psum.184 = f32[8,256]{1,0:T(8,128)S(1)} all-reduce(f32[8,256]{1,0:T(8,128)S(1)} %convolution_select_fusion.31), channel_id=1, replica_groups=mesh['dp'=32,'crow'=4,'ccol'=4] {'crow','ccol'}, use_global_device_ids=true, to_apply=%region_6.7 | all-reduce | flops 2048 | bytes 16384 | tf_op jit(solution)/shard_map/psum | solution.py:63
  137.0 1.4 fusion.49
  138.8 35.9 %psum.185 = f32[8,256]{1,0:T(8,128)S(1)} all-reduce(f32[8,256]{1,0:T(8,128)S(1)} %convolution_select_fusion.29), channel_id=1, replica_groups=mesh['dp'=32,'crow'=4,'ccol'=4] {'crow','ccol'}, use_global_device_ids=true, to_apply=%region_8.9 | all-reduce | flops 2048 | bytes 16384 | tf_op jit(solution)/shard_map/psum | solution.py:63
  174.8 0.9 fusion.48
  176.1 38.2 %psum.186 = f32[8,256]{1,0:T(8,128)S(1)} all-reduce(f32[8,256]{1,0:T(8,128)S(1)} %convolution_select_fusion.27), channel_id=1, replica_groups=mesh['dp'=32,'crow'=4,'ccol'=4] {'crow','ccol'}, use_global_device_ids=true, to_apply=%region_10.11 | all-reduce | flops 2048 | bytes 16384 | tf_op jit(solution)/shard_map/psum | solution.py:63
  214.2 0.9 fusion.47
  215.6 36.0 %psum.187 = f32[8,256]{1,0:T(8,128)S(1)} all-reduce(f32[8,256]{1,0:T(8,128)S(1)} %convolution_select_fusion.25), channel_id=1, replica_groups=mesh['dp'=32,'crow'=4,'ccol'=4] {'crow','ccol'}, use_global_device_ids=true, to_apply=%region_12.13 | all-reduce | flops 2048 | bytes 16384 | tf_op jit(solution)/shard_map/psum | solution.py:63
  251.5 0.8 fusion.46
  252.7 38.0 %psum.188 = f32[8,256]{1,0:T(8,128)S(1)} all-reduce(f32[8,256]{1,0:T(8,128)S(1)} %convolution_select_fusion.23), channel_id=1, replica_groups=mesh['dp'=32,'crow'=4,'ccol'=4] {'crow','ccol'}, use_global_device_ids=true, to_apply=%region_14.15 | all-reduce | flops 2048 | bytes 16384 | tf_op jit(solution)/shard_map/psum | solution.py:63
  290.7 0.8 fusion.45
  291.9 36.0 %psum.189 = f32[8,256]{1,0:T(8,128)S(1)} all-reduce(f32[8,256]{1,0:T(8,128)S(1)} %convolution_select_fusion.21), channel_id=1, replica_groups=mesh['dp'=32,'crow'=4,'ccol'=4] {'crow','ccol'}, use_global_device_ids=true, to_apply=%region_16.17 | all-reduce | flops 2048 | bytes 16384 | tf_op jit(solution)/shard_map/psum | solution.py:63
  327.9 0.8 fusion.44
  329.2 38.0 %psum.190 = f32[8,256]{1,0:T(8,128)S(1)} all-reduce(f32[8,256]{1,0:T(8,128)S(1)} %convolution_select_fusion.19), channel_id=1, replica_groups=mesh['dp'=32,'crow'=4,'ccol'=4] {'crow','ccol'}, use_global_device_ids=true, to_apply=%region_18.19 | all-reduce | flops 2048 | bytes 16384 | tf_op jit(solution)/shard_map/psum | solution.py:63
  367.2 0.8 fusion.43
  368.4 36.0 %psum.191 = f32[8,256]{1,0:T(8,128)S(1)} all-reduce(f32[8,256]{1,0:T(8,128)S(1)} %convolution_select_fusion.17), channel_id=1, replica_groups=mesh['dp'=32,'crow'=4,'ccol'=4] {'crow','ccol'}, use_global_device_ids=true, to_apply=%region_20.21 | all-reduce | flops 2048 | bytes 16384 | tf_op jit(solution)/shard_map/psum | solution.py:63
  404.4 0.8 fusion.42
  405.6 38.0 %psum.192 = f32[8,256]{1,0:T(8,128)S(1)} all-reduce(f32[8,256]{1,0:T(8,128)S(1)} %convolution_select_fusion.15), channel_id=1, replica_groups=mesh['dp'=32,'crow'=4,'ccol'=4] {'crow','ccol'}, use_global_device_ids=true, to_apply=%region_22.23 | all-reduce | flops 2048 | bytes 16384 | tf_op jit(solution)/shard_map/psum | solution.py:63
  443.6 0.8 fusion.41
  444.9 36.0 %psum.193 = f32[8,256]{1,0:T(8,128)S(1)} all-reduce(f32[8,256]{1,0:T(8,128)S(1)} %convolution_select_fusion.13), channel_id=1, replica_groups=mesh['dp'=32,'crow'=4,'ccol'=4] {'crow','ccol'}, use_global_device_ids=true, to_apply=%region_23.24 | all-reduce | flops 2048 | bytes 16384 | tf_op jit(solution)/shard_map/psum | solution.py:63
  480.8 0.8 fusion.40
  481.7 12.1 all_gather.6
  493.8 0.8 reshape.580
  494.6 0.9 copy.11
  495.6 12.0 while.45
  495.6 2.7 fusion.219
  498.5 3.1 fusion.220
  501.6 2.7 fusion.219
  504.5 3.1 fusion.220
  507.6 1.0 multiply_reduce_fusion.6
  508.7 55.2 %all-reduce.4.cloned.1.call-done = f32[2,8,1024]{2,1,0:T(8,128)} async-done(((f32[2,8,1024]{2,1,0:T(8,128)}), f32[2,8,1024]{2,1,0:T(8,128)}) %all-reduce.4.cloned.1.call-update) | async-done | bytes 65552 | tf_op jit(solution)/shard_map/psum | solution.py:79
  563.9 20.4 %while.46 = (s32[]{:T(128)}, f32[8,768]{1,0:T(8,128)}, f32[2,8,1024]{2,1,0:T(8,128)}, f32[16]{0:T(128)S(1)}, f32[16,768]{1,0:T(8,128)S(1)}, /*index=5*/f32[2,16,1024]{2,1,0:T(8,128)S(1)}, s32[]{:T(128)}, s32[]{:T(128)}) while((s32[]{:T(128)}, f32[8,768]{1,0:T(8,128)}, f32[2,8,1024]{2,1,0:T(8,128)}, f32[16]{0:T(128)S(1)}, ...), condition=%wide.region_32.33_spmd.clone, body=%wide.region_29.32_spmd.clone.sunk | while | flops 229763328 | bytes 6618855 | solution.py:85
  563.9 4.4 fusion.223
  568.5 5.6 fusion.224
  574.1 4.4 fusion.223
  578.6 5.6 fusion.224
  584.3 494.7 %psum.195 = f32[8,768]{1,0:T(8,128)S(1)} all-reduce(f32[8,768]{1,0:T(8,128)} %get-tuple-element.356), channel_id=1, replica_groups=mesh['dp'=32,'crow'=4,'ccol'=4] {'dp','crow'}, use_global_device_ids=true, to_apply=%region_33.34 | all-reduce | flops 6144 | bytes 49152 | tf_op jit(solution)/shard_map/psum | solution.py:88
  1079.0 11.8 all_gather.7
  1091.8 37.8 %psum.196 = f32[8,256]{1,0:T(8,128)S(1)} all-reduce(f32[8,256]{1,0:T(8,128)S(1)} %convolution_select_fusion.11), channel_id=1, replica_groups=mesh['dp'=32,'crow'=4,'ccol'=4] {'crow','ccol'}, use_global_device_ids=true, to_apply=%region_34.35 | all-reduce | flops 2048 | bytes 16384 | tf_op jit(solution)/shard_map/psum | solution.py:104
  1131.2 36.5 %psum.197 = f32[8,256]{1,0:T(8,128)S(1)} all-reduce(f32[8,256]{1,0:T(8,128)S(1)} %convolution_select_fusion.10), channel_id=1, replica_groups=mesh['dp'=32,'crow'=4,'ccol'=4] {'crow','ccol'}, use_global_device_ids=true, to_apply=%region_35.36 | all-reduce | flops 2048 | bytes 16384 | tf_op jit(solution)/shard_map/psum | solution.py:104
  1168.3 0.7 convolution_subtract_fusion.9
  1169.3 37.6 %psum.198 = f32[8,256]{1,0:T(8,128)S(1)} all-reduce(f32[8,256]{1,0:T(8,128)S(1)} %convolution_select_fusion.9), channel_id=1, replica_groups=mesh['dp'=32,'crow'=4,'ccol'=4] {'crow','ccol'}, use_global_device_ids=true, to_apply=%region_36.37 | all-reduce | flops 2048 | bytes 16384 | tf_op jit(solution)/shard_map/psum | solution.py:104
  1207.5 0.7 convolution_subtract_fusion.8
  1208.4 36.6 %psum.199 = f32[8,256]{1,0:T(8,128)S(1)} all-reduce(f32[8,256]{1,0:T(8,128)S(1)} %convolution_select_fusion.8), channel_id=1, replica_groups=mesh['dp'=32,'crow'=4,'ccol'=4] {'crow','ccol'}, use_global_device_ids=true, to_apply=%region_37.38 | all-reduce | flops 2048 | bytes 16384 | tf_op jit(solution)/shard_map/psum | solution.py:104
  1245.7 0.7 convolution_subtract_fusion.7
  1246.7 37.5 %psum.200 = f32[8,256]{1,0:T(8,128)S(1)} all-reduce(f32[8,256]{1,0:T(8,128)S(1)} %convolution_select_fusion.7), channel_id=1, replica_groups=mesh['dp'=32,'crow'=4,'ccol'=4] {'crow','ccol'}, use_global_device_ids=true, to_apply=%region_38.39 | all-reduce | flops 2048 | bytes 16384 | tf_op jit(solution)/shard_map/psum | solution.py:104
  1284.8 0.7 convolution_subtract_fusion.6
  1285.8 36.5 %psum.201 = f32[8,256]{1,0:T(8,128)S(1)} all-reduce(f32[8,256]{1,0:T(8,128)S(1)} %convolution_select_fusion.6), channel_id=1, replica_groups=mesh['dp'=32,'crow'=4,'ccol'=4] {'crow','ccol'}, use_global_device_ids=true, to_apply=%region_39.40 | all-reduce | flops 2048 | bytes 16384 | tf_op jit(solution)/shard_map/psum | solution.py:104
  1323.0 0.7 convolution_subtract_fusion.5
  1324.0 37.5 %psum.202 = f32[8,256]{1,0:T(8,128)S(1)} all-reduce(f32[8,256]{1,0:T(8,128)S(1)} %convolution_select_fusion.5), channel_id=1, replica_groups=mesh['dp'=32,'crow'=4,'ccol'=4] {'crow','ccol'}, use_global_device_ids=true, to_apply=%region_40.41 | all-reduce | flops 2048 | bytes 16384 | tf_op jit(solution)/shard_map/psum | solution.py:104
  1362.1 0.7 convolution_subtract_fusion.4
  1363.1 36.5 %psum.203 = f32[8,256]{1,0:T(8,128)S(1)} all-reduce(f32[8,256]{1,0:T(8,128)S(1)} %convolution_select_fusion.4), channel_id=1, replica_groups=mesh['dp'=32,'crow'=4,'ccol'=4] {'crow','ccol'}, use_global_device_ids=true, to_apply=%region_41.42 | all-reduce | flops 2048 | bytes 16384 | tf_op jit(solution)/shard_map/psum | solution.py:104
  1400.3 0.7 convolution_subtract_fusion.3
  1401.3 37.6 %psum.204 = f32[8,256]{1,0:T(8,128)S(1)} all-reduce(f32[8,256]{1,0:T(8,128)S(1)} %convolution_select_fusion.3), channel_id=1, replica_groups=mesh['dp'=32,'crow'=4,'ccol'=4] {'crow','ccol'}, use_global_device_ids=true, to_apply=%region_42.43 | all-reduce | flops 2048 | bytes 16384 | tf_op jit(solution)/shard_map/psum | solution.py:104
  1440.5 36.5 %psum.205 = f32[8,256]{1,0:T(8,128)S(1)} all-reduce(f32[8,256]{1,0:T(8,128)S(1)} %convolution_select_fusion.2), channel_id=1, replica_groups=mesh['dp'=32,'crow'=4,'ccol'=4] {'crow','ccol'}, use_global_device_ids=true, to_apply=%region_43.44 | all-reduce | flops 2048 | bytes 16384 | tf_op jit(solution)/shard_map/psum | solution.py:104
  1478.6 37.5 %psum.206 = f32[8,256]{1,0:T(8,128)S(1)} all-reduce(f32[8,256]{1,0:T(8,128)S(1)} %convolution_select_fusion.1), channel_id=1, replica_groups=mesh['dp'=32,'crow'=4,'ccol'=4] {'crow','ccol'}, use_global_device_ids=true, to_apply=%region_44.45 | all-reduce | flops 2048 | bytes 16384 | tf_op jit(solution)/shard_map/psum | solution.py:104
  1517.8 36.5 %psum.207 = f32[8,256]{1,0:T(8,128)S(1)} all-reduce(f32[8,256]{1,0:T(8,128)S(1)} %convolution_select_fusion), channel_id=1, replica_groups=mesh['dp'=32,'crow'=4,'ccol'=4] {'crow','ccol'}, use_global_device_ids=true, to_apply=%region_45.46 | all-reduce | flops 2048 | bytes 16384 | tf_op jit(solution)/shard_map/psum | solution.py:104
  1554.4 1.1 multiply_reduce_fusion.4
  1555.5 1.7 multiply_add_fusion
  (84 shorter events, 26.4 us)
Async XLA Ops:
  7.2 91.3 %copy-start = (f32[768,768]{1,0:T(8,128)S(1)}, f32[768,768]{1,0:T(8,128)}, u32[]{:S(2)}) copy-start(f32[768,768]{1,0:T(8,128)} %param.63) | copy-start | bytes 7077892
  7.2 129.8 %copy-start.1 = (f32[3,256,256]{2,1,0:T(8,128)S(1)}, f32[3,256,256]{2,1,0:T(8,128)}, u32[]{:S(2)}) copy-start(f32[3,256,256]{2,1,0:T(8,128)} %param.64) | copy-start | bytes 2359300
  7.2 167.6 %copy-start.3 = (f32[8,3072]{1,0:T(8,128)S(1)}, f32[8,3072]{1,0:T(8,128)}, u32[]{:S(2)}) copy-start(f32[8,3072]{1,0:T(8,128)} %param.67) | copy-start | bytes 294916
  7.2 556.7 %all-reduce.4.cloned.1.call-start = ((), (), s32[]{:S(2)}) async-start(), calls=%async_computation | async-start | bytes 131072 | tf_op jit(solution)/shard_map/psum | solution.py:79
  328.7 165.1 %copy-start.6 = (f32[16,2048]{1,0:T(8,128)S(1)}, f32[16,2048]{1,0:T(8,128)}, u32[]{:S(2)}) copy-start(f32[16,2048]{1,0:T(8,128)} %param.60) | copy-start | bytes 393220
  329.2 166.4 %copy-start.2 = (f32[16,768]{1,0:T(8,128)S(1)}, f32[16,768]{1,0:T(8,128)}, u32[]{:S(2)}) copy-start(f32[16,768]{1,0:T(8,128)} %param.61) | copy-start | bytes 147460
  329.2 166.4 %copy-start.4 = (f32[16]{0:T(128)S(1)}, f32[16]{0:T(128)}, u32[]{:S(2)}) copy-start(f32[16]{0:T(128)} %param.62) | copy-start | bytes 196
  1555.5 1.7 copy-start.5
Sparse Core Ops, SparseCore 0:
  507.7 56.0 all-reduce.3
where the time goes:
time: 1570 us; the launch traced here: 1560 us
  blocking collectives  1410 us (90%)
  matrix products  62.8 us (4%)
  waiting for transfers between devices  55.2 us (4%)
  other arithmetic  18.8 us (1%)
    psum x1, blocking collectives, per_device(): summed = lax.psum(summed, ('dp', 'crow'))  495 us
    psum x12, blocking collectives, per_device(): partial_value = lax.psum(partial_value, ('crow', 'ccol'))  448 us
    psum x12, blocking collectives, per_device(): piece = lax.psum(term, ('crow', 'ccol'))  445 us
    psum x1, waiting for transfers between devices, per_device(): images = lax.psum(images, 'ccol')  55.2 us
  transfers between devices with their start and end apart: 1, of which 1 were waited for; matrix products, arithmetic and copies ran while one was open for 0% of the time, Pallas kernels for 0%

commit v1 on v0

v1 whole, which is shorter than its diff:
```python
import functools

import jax
import jax.numpy as jnp
from jax import lax
from jax.experimental import pallas as pl
from jax.experimental.pallas import tpu as pltpu
from jax.sharding import PartitionSpec as P

MESH = pl.DeviceIdType.MESH
f32 = jnp.float32
bf16 = jnp.bfloat16
HIGHEST = lax.Precision.HIGHEST
ridge_weight = 0.2

NN = (((1,), (0,)), ((), ()))
NT = (((1,), (1,)), ((), ()))
TN = (((0,), (0,)), ((), ()))


def dot(a, b, dims=NN, precision=None):
    return lax.dot_general(a, b, dims, precision=precision, preferred_element_type=f32)


def split2(v):
    high = v.astype(bf16)
    return high, (v - high.astype(f32)).astype(bf16)


def split3(v):
    high = v.astype(bf16)
    rest = v - high.astype(f32)
    mid = rest.astype(bf16)
    return high, mid, (rest - mid.astype(f32)).astype(bf16)


def product(v, high, low, dims=NN):
    rows = v.shape[0]
    both = jnp.concatenate(split2(v), axis=0)
    out = dot(both, low, dims) + dot(both, high, dims)
    return out[rows:] + out[:rows]


def ring_distance(d, n):
    d = d % n
    return min(d, n - d)


class Semaphores:
    def __init__(self):
        self.count = 0

    def take(self, n):
        first = self.count
        self.count += n
        return first


S = Semaphores()
LOAD = S.take(8)
CEN_R = S.take(4)
CEN_S = S.take(3)
CENF_S = S.take(4)
P_R = S.take(4)
P_S = S.take(16)
PF_S = S.take(4)
PROD_R = S.take(4)
PROD_S = S.take(1)
N_R = S.take(1)
N_S = S.take(16)
Z_R = S.take(1)
Z_S = S.take(16)
M_R = S.take(3)
M_S = S.take(1)
IMG_R = S.take(4)
IMG_S = S.take(16)
IMGF_S = S.take(4)
BACK_R = S.take(4)
BACK_S = S.take(1)


def kernel(
    planes,
    total_rows,
    data,
    centres,
    scales,
    factor,
    block_inv,
    iterate,
    residual,
    direction,
    new_iterate,
    new_residual,
    new_direction,
    fac,
    inv,
    whi,
    wlo,
    thi,
    tlo,
    rows,
    cen,
    khi,
    klo,
    itv,
    rev,
    div,
    pulled,
    prod_out,
    prod_in,
    nsend,
    nred,
    zred,
    mout,
    min_,
    img,
    back_out,
    back_in,
    sems,
    zready,
):
    dp = lax.axis_index("dp")
    r = lax.axis_index("crow")
    c = lax.axis_index("ccol")
    core = lax.rem(dp, 2)
    z = dp // 2
    solver = core == 1
    width = fac.shape[0]
    span = rows.shape[1]
    order = inv.shape[1]
    pending = []

    def local(src, dst, k):
        return pltpu.make_async_copy(src, dst, sems.at[LOAD + k])

    def remote(src, dst, ss, rs, dev):
        return pltpu.make_async_remote_copy(
            src_ref=src,
            dst_ref=dst,
            send_sem=sems.at[ss],
            recv_sem=sems.at[rs],
            device_id=dev,
            device_id_type=MESH,
        )

    def arrived(dst, rs):
        pltpu.make_async_copy(dst, dst, sems.at[rs]).wait()

    def send(cond, src, dst, ss, rs, dev):
        remote(src(), dst(), ss, rs, dev).start()
        pending.append((cond, src, ss))

    load_fac = local(factor, fac, 0)
    load_inv = local(block_inv, inv, 1)
    load_dir = local(direction, div, 2)
    load_cen = local(centres, cen.at[c], 3)
    load_rows = local(data.at[:, pl.ds(pl.multiple_of(c * span, 128), span)], rows, 4)
    load_res = local(residual, rev, 5)
    load_it = local(iterate, itv, 6)
    diagonal = solver & (r == c)
    below = solver & (r > c)

    @pl.when(diagonal)
    def _():
        load_inv.start()

    load_dir.start()

    @pl.when(diagonal | below)
    def _():
        load_fac.start()

    load_cen.start()
    load_rows.start()
    load_res.start()
    load_it.start()

    barrier = pltpu.get_barrier_semaphore()
    near = sorted({d % planes for d in (1, 2, 3, 4, -1, -2, -3, -4)} - {0})
    relay = sorted({d % planes for d in (4, -4)}) if planes > 9 else []
    offsets = sorted(
        [(a, b) for a in range(4) for b in range(4)],
        key=lambda o: (-ring_distance(o[0], 4) - ring_distance(o[1], 4), o),
    )

    def signal(sem, dev):
        pl.semaphore_signal(sem, inc=1, device_id=dev, device_id_type=MESH)

    @pl.when(solver)
    def _():
        for a, b in offsets[:-1]:
            signal(barrier, (dp, lax.rem(r + a, 4), lax.rem(c + b, 4)))
        for d in near:
            signal(barrier, (2 * lax.rem(z + d, planes) + 1, r, c))
        signal(barrier, (dp - 1, r, c))

    @pl.when(core == 0)
    def _():
        signal(barrier, (dp + 1, r, c))

    load_dir.wait()

    first = solver & (r == 3) & (c == 3)

    @pl.when(first)
    def _():
        load_inv.wait()
        load_fac.wait()
        b = [slice(k * order, (k + 1) * order) for k in range(3)]
        base = 3 * width
        d = [div[:, base + k * order : base + (k + 1) * order] for k in range(3)]
        p2 = dot(d[2], inv[2], NN, HIGHEST)
        p1 = dot(d[1] - dot(p2, fac[b[2], b[1]], NN, HIGHEST), inv[1], NN, HIGHEST)
        t0 = d[0] - dot(p2, fac[b[2], b[0]], NN, HIGHEST)
        p0 = dot(t0 - dot(p1, fac[b[1], b[0]], NN, HIGHEST), inv[0], NN, HIGHEST)
        pulled[3, :, b[0]] = p0
        pulled[3, :, b[1]] = p1
        pulled[3, :, b[2]] = p2

    def keep(v, i, j):
        si = slice(i * order, (i + 1) * order)
        sj = slice(j * order, (j + 1) * order)
        whi[si, sj], wlo[si, sj] = split2(v)
        thi[sj, si], tlo[sj, si] = split2(v.T)

    @pl.when(below)
    def _():
        load_fac.wait()
        for i in range(3):
            for j in range(3):
                keep(fac[i * order : (i + 1) * order, j * order : (j + 1) * order], i, j)

    @pl.when(solver)
    def _():
        pl.semaphore_wait(barrier, 15 + len(near) + 1)
        for d in relay:
            signal(zready, (2 * lax.rem(z + d, planes) + 1, r, c))

    @pl.when(core == 0)
    def _():
        pl.semaphore_wait(barrier, 1)

    def spread(k, cond, buf, ss, rs, urgent):
        rest = [o for o in offsets[:-1] if ((k + o[0]) % 4, (k + o[1]) % 4) not in urgent]
        goals = urgent + [((k + a) % 4, (k + b) % 4) for a, b in rest]
        for i, (a, b) in enumerate(goals):
            send(cond, lambda: buf.at[k], lambda: buf.at[k], ss + i, rs + k, (dp, a, b))

    def give_core0(cond, buf, k, ss, rs):
        send(cond, lambda: buf.at[k], lambda: buf.at[k], ss + k, rs + k, (dp - 1, r, c))

    @pl.when(first)
    def _():
        spread(3, first, pulled, P_S, P_R, [(3, 2), (3, 1), (3, 0)])

    load_cen.wait()

    @pl.when(solver)
    def _():
        for i, d in enumerate((2, 1, 3)):
            send(solver, lambda: cen.at[c], lambda: cen.at[c], CEN_S + i, CEN_R + c, (dp, r, lax.rem(c + d, 4)))

    def invert():
        b = [slice(k * order, (k + 1) * order) for k in range(3)]
        mul = functools.partial(dot, precision=HIGHEST)
        zero = jnp.zeros((order, order), f32)
        a0, a1, a2 = inv[0], inv[1], inv[2]
        x10 = -mul(a1, mul(fac[b[1], b[0]], a0))
        x21 = -mul(a2, mul(fac[b[2], b[1]], a1))
        x20 = -mul(a2, mul(fac[b[2], b[0]], a0) + mul(fac[b[2], b[1]], x10))
        for i, row in enumerate(((a0, zero, zero), (x10, a1, zero), (x20, x21, a2))):
            for j, v in enumerate(row):
                keep(v, i, j)

    @pl.when(diagonal & (r != 3))
    def _():
        load_inv.wait()
        load_fac.wait()
        invert()

    scale_col = jnp.zeros((rows.shape[0], 1), f32)
    place = lax.broadcasted_iota(jnp.int32, (rows.shape[0], 1), 0)
    for k in range(rows.shape[0]):
        scale_col = jnp.where(place == k, scales[k], scale_col)

    load_rows.wait()

    for i, d in enumerate((1, 3, 2)):
        src = lax.rem(c + d, 4)
        arrived(cen.at[src], CEN_R + src)

        @pl.when(solver)
        def _():
            send(solver, lambda src=src: cen.at[src], lambda src=src: cen.at[src], CENF_S + i, CEN_R + src, (dp - 1, r, c))

    def tiles():
        x = rows[...] / scale_col
        xh, xm, xl = split3(x)
        right = jnp.concatenate([xh, xm, xh, xl, xh, xm], axis=0)
        xn = -0.5 * jnp.sum(x * x, axis=0)[None, :]
        for k in range(4):
            for q in range(3):
                m = cen[k, :, q * order : (q + 1) * order] / scale_col
                mh, mm, ml = split3(m)
                left = jnp.concatenate([mh, mh, mm, mh, ml, mm], axis=0)
                mn = -0.5 * jnp.sum(m * m, axis=0)[:, None]
                v = jnp.exp(dot(left, right, TN) + mn + xn)
                at = slice(k * width + q * order, k * width + (q + 1) * order)
                khi[at, :], klo[at, :] = split2(v)

    @pl.when((r != 3) | (core == 0))
    def _():
        tiles()

    images = jnp.zeros((div.shape[0], span), f32)

    for k in (3, 2, 1, 0):
        mine = solver & (r == k) & (c == k)

        if k < 3:

            @pl.when(mine)
            def _():
                t = div[:, k * width : (k + 1) * width]
                for j in range(3, k, -1):
                    arrived(prod_in.at[j], PROD_R + j)
                    t = t - prod_in[j]
                pulled[k] = product(t, whi[...], wlo[...])
                spread(k, mine, pulled, P_S, P_R, [(k, j) for j in range(k - 1, -1, -1)])

        @pl.when(jnp.logical_not(mine))
        def _():
            arrived(pulled.at[k], P_R + k)

        multiply = solver & (r == k) & (c < k)

        if k > 0:

            @pl.when(multiply)
            def _():
                prod_out[...] = product(pulled[k], whi[...], wlo[...])
                send(multiply, lambda: prod_out, lambda: prod_in.at[k], PROD_S, PROD_R + k, (dp, c, c))

        @pl.when(solver)
        def _():
            give_core0(solver, pulled, k, PF_S, P_R)

        if k == 3:

            @pl.when((r == 3) & solver)
            def _():
                tiles()

            @pl.when(first)
            def _():
                invert()

        at = slice(k * width, (k + 1) * width)
        images = images + product(pulled[k], khi[at, :], klo[at, :])

    both = jnp.concatenate(split2(images), axis=0)
    rhs = div.shape[0]
    for i, (a, b) in enumerate(offsets):
        x = lax.rem(r + a, 4)
        y = lax.rem(c + b, 4)
        gap = lax.rem(y - x + 4, 4)
        owned = gap != 2
        chunk = 3 * x + jnp.where(gap == 3, 2, gap)
        slot = 2 * i + core

        @pl.when(owned)
        def _():
            at = pl.ds(pl.multiple_of(chunk * order, order), order)
            out = dot(both, klo[at, :], NT) + dot(both, khi[at, :], NT)
            nsend[chunk] = out[rhs:] + out[:rhs]

        if i < 15:

            @pl.when(owned)
            def _():
                send(owned, lambda chunk=chunk: nsend.at[chunk], lambda: nred.at[slot], N_S + i, N_R, (2 * z + 1, x, y))

        else:

            @pl.when(owned & solver)
            def _():
                nred[31] = nsend[chunk]

            away = owned & (core == 0)

            @pl.when(away)
            def _():
                send(away, lambda chunk=chunk: nsend.at[chunk], lambda: nred.at[30], N_S + i, N_R, (2 * z + 1, x, y))

    gap = lax.rem(c - r + 4, 4)
    owner = solver & (gap != 2)
    part = jnp.where(gap == 3, 2, gap)

    if relay:

        @pl.when(solver)
        def _():
            pl.semaphore_wait(zready, len(relay))

    far = sorted(range(1, planes), key=lambda d: -ring_distance(d, planes))

    @pl.when(owner)
    def _():
        arrived(nred.at[0:31], N_R)
        total = nred[0]
        for s in range(1, 32):
            total = total + nred[s]
        zred[z] = total
        for i, d in enumerate(far):
            send(
                owner,
                lambda: zred.at[z],
                lambda: zred.at[z],
                Z_S + i,
                Z_R,
                (2 * lax.rem(z + d, planes) + 1, r, c),
            )
        arrived(zred.at[0 : planes - 1], Z_R)
        total = zred[0]
        for s in range(1, planes):
            total = total + zred[s]
        mout[...] = total * (1.0 / total_rows)

    passing = owner & (gap != 0)

    @pl.when(passing)
    def _():
        send(passing, lambda: mout, lambda: min_.at[part], M_S, M_R + part, (dp, r, r))

    @pl.when(diagonal)
    def _():
        min_[0] = mout[...]
        arrived(min_.at[1], M_R + 1)
        arrived(min_.at[2], M_R + 2)

    for k in range(4):
        mine = solver & (r == k) & (c == k)

        @pl.when(mine)
        def _():
            t = jnp.concatenate([min_[0], min_[1], min_[2]], axis=1) + ridge_weight * pulled[k]
            for j in range(k):
                arrived(back_in.at[j], BACK_R + j)
                t = t - back_in[j]
            img[k] = product(t, thi[...], tlo[...])
            spread(k, mine, img, IMG_S, IMG_R, [(j, k) for j in range(k + 1, 4)])

        @pl.when(jnp.logical_not(mine))
        def _():
            arrived(img.at[k], IMG_R + k)

        multiply = solver & (c == k) & (r > k)

        if k < 3:

            @pl.when(multiply)
            def _():
                back_out[...] = product(img[k], thi[...], tlo[...])
                send(multiply, lambda: back_out, lambda: back_in.at[k], BACK_S, BACK_R + k, (dp, r, r))

        @pl.when(solver)
        def _():
            give_core0(solver, img, k, IMGF_S, IMG_R)

    load_res.wait()
    load_it.wait()
    gamma = jnp.sum(rev[...] * rev[...], axis=1, keepdims=True)
    segs = [slice(k * width, (k + 1) * width) for k in range(4)]
    curvature = jnp.zeros((rhs, 1), f32)
    for k in range(4):
        curvature += jnp.sum(div[:, segs[k]] * img[k], axis=1, keepdims=True)
    alpha = gamma / curvature
    gamma_next = jnp.zeros((rhs, 1), f32)
    for k in range(4):
        res = rev[:, segs[k]] - alpha * img[k]
        new_residual[:, segs[k]] = res
        gamma_next += jnp.sum(res * res, axis=1, keepdims=True)
    new_iterate[...] = itv[...] + alpha * div[...]
    new_direction[...] = new_residual[...] + (gamma_next / gamma) * div[...]

    for cond, src, ss in pending:

        @pl.when(cond)
        def _():
            arrived(src(), ss)


def per_device(data, centres, scales, factor, block_inv, iterate, residual, direction):
    planes = lax.axis_size("dp") // 2
    total_rows = data.shape[1] * lax.axis_size("dp") * lax.axis_size("crow")
    inputs, width = centres.shape
    span = data.shape[1] // lax.axis_size("ccol")
    rhs, total = direction.shape
    order = block_inv.shape[1]
    whole = jax.ShapeDtypeStruct((rhs, total), f32)
    vmem = pltpu.VMEM
    hbm = pl.BlockSpec(memory_space=pl.ANY)
    square = (width, width)
    return pl.pallas_call(
        functools.partial(kernel, planes, total_rows),
        out_shape=(whole, whole, whole),
        in_specs=[hbm, hbm, pl.BlockSpec(memory_space=pltpu.SMEM)] + [hbm] * 5,
        out_specs=(pl.BlockSpec(memory_space=pltpu.VMEM),) * 3,
        scratch_shapes=[
            vmem(square, f32),
            vmem((3, order, order), f32),
            vmem(square, bf16),
            vmem(square, bf16),
            vmem(square, bf16),
            vmem(square, bf16),
            vmem((inputs, span), f32),
            vmem((4, inputs, width), f32),
            vmem((total, span), bf16),
            vmem((total, span), bf16),
            vmem((rhs, total), f32),
            vmem((rhs, total), f32),
            vmem((rhs, total), f32),
            vmem((4, rhs, width), f32),
            vmem((rhs, width), f32),
            vmem((4, rhs, width), f32),
            vmem((12, rhs, order), f32),
            vmem((32, rhs, order), f32),
            vmem((planes, rhs, order), f32),
            vmem((rhs, order), f32),
            vmem((3, rhs, order), f32),
            vmem((4, rhs, width), f32),
            vmem((rhs, width), f32),
            vmem((4, rhs, width), f32),
            pltpu.SemaphoreType.DMA((S.count,)),
            pltpu.SemaphoreType.REGULAR,
        ],
        compiler_params=pltpu.CompilerParams(
            collective_id=0, has_side_effects=True, vmem_limit_bytes=50 * 1024 * 1024
        ),
    )(data, centres, scales, factor, block_inv, iterate, residual, direction)


def solution(mesh):
    placed = (
        P(None, ("dp", "crow")),
        P(None, "ccol"),
        P(),
        P("crow", "ccol"),
        P("crow", None, None),
        P(),
        P(),
        P(),
    )
    return jax.shard_map(
        per_device, mesh=mesh, in_specs=placed, out_specs=(P(), P(), P()), check_vma=False
    )
```

time: 1570 us -> 82.3 us (0.05)
  the two profiles are of different devices: /device:TPU:8 before, /device:TPU:1 now
where the time goes in v1:
time: 82.3 us; the launch traced here: 81.9 us
  Pallas kernels  71.5 us (87%)
  local copies, waits for them, and re-layouts  9.75 us (12%)
    pallas_call x1, Pallas kernels, per_device(): pl.pallas_call(functools.partial(kernel, planes, total_rows), out_shape=(...  71.5 us
    unnamed x19, local copies, waits for them, and re-layouts  9.75 us

profile of v1, /device:TPU:1, one launch (start us, length us, event | category | flops | bytes accessed | tf_op | source)
XLA Modules:
  0.0 81.9 jit_solution(11528947769399202715)
XLA Ops:
  0.6 0.0 copy-start
  0.6 1.7 %copy-done = f32[768,768]{1,0:T(8,128)S(1)} copy-done((f32[768,768]{1,0:T(8,128)S(1)}, f32[768,768]{1,0:T(8,128)}, u32[]{:S(2)}) %copy-start) | copy-done | bytes 2359320
  2.3 0.0 copy-start.1
  2.3 1.1 %copy-done.1 = f32[3,256,256]{2,1,0:T(8,128)S(1)} copy-done((f32[3,256,256]{2,1,0:T(8,128)S(1)}, f32[3,256,256]{2,1,0:T(8,128)}, u32[]{:S(2)}) %copy-start.1) | copy-done | bytes 786456
  3.4 0.0 copy-start.2
  3.4 0.9 %copy-done.2 = f32[16,2048]{1,0:T(8,128)S(1)} copy-done((f32[16,2048]{1,0:T(8,128)S(1)}, f32[16,2048]{1,0:T(8,128)}, u32[]{:S(2)}) %copy-start.2) | copy-done | bytes 131096
  4.3 0.0 copy-start.3
  4.3 0.9 %copy-done.3 = f32[8,3072]{1,0:T(8,128)S(1)} copy-done((f32[8,3072]{1,0:T(8,128)S(1)}, f32[8,3072]{1,0:T(8,128)}, u32[]{:S(2)}) %copy-start.3) | copy-done | bytes 98328
  5.2 0.0 copy-start.4
  5.2 0.9 %copy-done.4 = f32[8,3072]{1,0:T(8,128)S(1)} copy-done((f32[8,3072]{1,0:T(8,128)S(1)}, f32[8,3072]{1,0:T(8,128)}, u32[]{:S(2)}) %copy-start.4) | copy-done | bytes 98328
  6.1 0.0 copy-start.5
  6.1 0.9 %copy-done.5 = f32[8,3072]{1,0:T(8,128)S(1)} copy-done((f32[8,3072]{1,0:T(8,128)S(1)}, f32[8,3072]{1,0:T(8,128)}, u32[]{:S(2)}) %copy-start.5) | copy-done | bytes 98328
  7.0 0.0 copy-start.6
  7.0 0.8 copy-done.6
  7.8 0.0 copy-start.7
  7.8 0.7 copy-done.7
  8.5 71.5 %shard_map.103 = (f32[8,3072]{1,0:T(8,128)S(1)}, f32[8,3072]{1,0:T(8,128)S(1)}, f32[8,3072]{1,0:T(8,128)S(1)}) custom-call(f32[16,2048]{1,0:T(8,128)S(1)} %copy-done.2, f32[16,768]{1,0:T(8,128)S(1)} %copy-done.6, f32[16]{0:T(128)S(1)} %copy-done.7, f32[768,768]{1,0:T(8,128)S(1)} %copy-done, f32[3,256,256]{2,1,0:T(8,128)S(1)} %copy-done.1, ...), custom_call_target="tpu_custom_call" | custom-call | tf_op jit(solution)/shard_map/pallas_call | solution.py:505
  80.0 0.6 copy.14
  80.6 0.6 copy.15
  81.3 0.6 copy.16
Async XLA Ops:
  0.6 1.7 %copy-start = (f32[768,768]{1,0:T(8,128)S(1)}, f32[768,768]{1,0:T(8,128)}, u32[]{:S(2)}) copy-start(f32[768,768]{1,0:T(8,128)} %factor.1) | copy-start | bytes 7077892
  2.3 1.1 %copy-start.1 = (f32[3,256,256]{2,1,0:T(8,128)S(1)}, f32[3,256,256]{2,1,0:T(8,128)}, u32[]{:S(2)}) copy-start(f32[3,256,256]{2,1,0:T(8,128)} %block_inv.1) | copy-start | bytes 2359300
  3.4 0.9 %copy-start.2 = (f32[16,2048]{1,0:T(8,128)S(1)}, f32[16,2048]{1,0:T(8,128)}, u32[]{:S(2)}) copy-start(f32[16,2048]{1,0:T(8,128)} %data.1) | copy-start | bytes 393220
  4.3 0.9 %copy-start.3 = (f32[8,3072]{1,0:T(8,128)S(1)}, f32[8,3072]{1,0:T(8,128)}, u32[]{:S(2)}) copy-start(f32[8,3072]{1,0:T(8,128)} %iterate.1) | copy-start | bytes 294916
  5.2 0.9 %copy-start.4 = (f32[8,3072]{1,0:T(8,128)S(1)}, f32[8,3072]{1,0:T(8,128)}, u32[]{:S(2)}) copy-start(f32[8,3072]{1,0:T(8,128)} %residual.1) | copy-start | bytes 294916
  6.1 0.9 %copy-start.5 = (f32[8,3072]{1,0:T(8,128)S(1)}, f32[8,3072]{1,0:T(8,128)}, u32[]{:S(2)}) copy-start(f32[8,3072]{1,0:T(8,128)} %direction.1) | copy-start | bytes 294916
  7.0 0.8 copy-start.6
  7.8 0.7 copy-start.7

commit v2 on v1

--- a/solution.py
+++ b/solution.py
@@ -41,6 +41,18 @@
     return out[rows:] + out[:rows]
 
 
+def lower(v, high, low, order):
+    parts = [product(v[:, j:], high[j:, j : j + order], low[j:, j : j + order]) for j in range(0, v.shape[1], order)]
+    return jnp.concatenate(parts, axis=1)
+
+
+def upper(v, high, low, order):
+    parts = []
+    for j in range(0, v.shape[1], order):
+        parts.append(product(v[:, : j + order], high[: j + order, j : j + order], low[: j + order, j : j + order]))
+    return jnp.concatenate(parts, axis=1)
+
+
 def ring_distance(d, n):
     d = d % n
     return min(d, n - d)
@@ -55,6 +67,10 @@
         self.count += n
         return first
 
+
+OWNERS = ((1, 0), (0, 0), (2, 0), (1, 1), (1, 3), (0, 1), (3, 2), (2, 2), (0, 2), (3, 3), (3, 1), (2, 3))
+LOW = (1, 0)
+HIGH = (3, 2)
 
 S = Semaphores()
 LOAD = S.take(8)
@@ -70,13 +86,15 @@
 N_S = S.take(16)
 Z_R = S.take(1)
 Z_S = S.take(16)
-M_R = S.take(3)
+M_R = S.take(6)
 M_S = S.take(1)
 IMG_R = S.take(4)
-IMG_S = S.take(16)
+IMG_S = S.take(30)
 IMGF_S = S.take(4)
 BACK_R = S.take(4)
 BACK_S = S.take(1)
+BULK_R = S.take(6)
+BULK_S = S.take(3)
 
 
 def kernel(
@@ -87,12 +105,11 @@
     scales,
     factor,
     block_inv,
-    iterate,
     residual,
     direction,
-    new_iterate,
-    new_residual,
-    new_direction,
+    image,
+    alphas,
+    betas,
     fac,
     inv,
     whi,
@@ -103,7 +120,6 @@
     cen,
     khi,
     klo,
-    itv,
     rev,
     div,
     pulled,
@@ -117,6 +133,9 @@
     img,
     back_out,
     back_in,
+    aux,
+    dhi,
+    dlo,
     sems,
     zready,
 ):
@@ -157,9 +176,9 @@
     load_cen = local(centres, cen.at[c], 3)
     load_rows = local(data.at[:, pl.ds(pl.multiple_of(c * span, 128), span)], rows, 4)
     load_res = local(residual, rev, 5)
-    load_it = local(iterate, itv, 6)
     diagonal = solver & (r == c)
     below = solver & (r > c)
+    holders = [solver & (r == k) & (c == k) for k in range(4)]
 
     @pl.when(diagonal)
     def _():
@@ -174,7 +193,6 @@
     load_cen.start()
     load_rows.start()
     load_res.start()
-    load_it.start()
 
     barrier = pltpu.get_barrier_semaphore()
     near = sorted({d % planes for d in (1, 2, 3, 4, -1, -2, -3, -4)} - {0})
@@ -241,18 +259,33 @@
     def _():
         pl.semaphore_wait(barrier, 1)
 
-    def spread(k, cond, buf, ss, rs, urgent):
-        rest = [o for o in offsets[:-1] if ((k + o[0]) % 4, (k + o[1]) % 4) not in urgent]
-        goals = urgent + [((k + a) % 4, (k + b) % 4) for a, b in rest]
+    def spread(source, k, cond, buf, ss, rs, urgent, first=0, last=15):
+        goals = [((source[0] + a) % 4, (source[1] + b) % 4) for a, b in offsets[:-1]]
+        goals = urgent + [g for g in goals if g not in urgent]
         for i, (a, b) in enumerate(goals):
-            send(cond, lambda: buf.at[k], lambda: buf.at[k], ss + i, rs + k, (dp, a, b))
+            if first <= i < last:
+                send(cond, lambda: buf.at[k], lambda: buf.at[k], ss + i, rs + k, (dp, a, b))
+
+    def give_inverse(k):
+        cond = holders[k]
+        goal = LOW if k < 2 else HIGH
+        for i in range(3):
+            at = (slice(i * order, (i + 1) * order), slice(0, (i + 1) * order))
+            send(
+                cond,
+                lambda at=at: fac.at[at],
+                lambda: aux.at[(k % 2,) + at],
+                BULK_S + i,
+                BULK_R + 3 * (k % 2) + i,
+                (dp,) + goal,
+            )
 
     def give_core0(cond, buf, k, ss, rs):
         send(cond, lambda: buf.at[k], lambda: buf.at[k], ss + k, rs + k, (dp - 1, r, c))
 
     @pl.when(first)
     def _():
-        spread(3, first, pulled, P_S, P_R, [(3, 2), (3, 1), (3, 0)])
+        spread((3, 3), 3, first, pulled, P_S, P_R, [(3, 2), (3, 1), (3, 0)])
 
     load_cen.wait()
 
@@ -264,20 +297,24 @@
     def invert():
         b = [slice(k * order, (k + 1) * order) for k in range(3)]
         mul = functools.partial(dot, precision=HIGHEST)
-        zero = jnp.zeros((order, order), f32)
         a0, a1, a2 = inv[0], inv[1], inv[2]
         x10 = -mul(a1, mul(fac[b[1], b[0]], a0))
         x21 = -mul(a2, mul(fac[b[2], b[1]], a1))
         x20 = -mul(a2, mul(fac[b[2], b[0]], a0) + mul(fac[b[2], b[1]], x10))
-        for i, row in enumerate(((a0, zero, zero), (x10, a1, zero), (x20, x21, a2))):
+        for i, row in enumerate(((a0,), (x10, a1), (x20, x21, a2))):
             for j, v in enumerate(row):
-                keep(v, i, j)
+                fac[b[i], b[j]] = v
+                whi[b[i], b[j]], wlo[b[i], b[j]] = split2(v)
 
     @pl.when(diagonal & (r != 3))
     def _():
         load_inv.wait()
         load_fac.wait()
         invert()
+
+    @pl.when(diagonal & (r == 0))
+    def _():
+        give_inverse(0)
 
     scale_col = jnp.zeros((rows.shape[0], 1), f32)
     place = lax.broadcasted_iota(jnp.int32, (rows.shape[0], 1), 0)
@@ -315,6 +352,13 @@
 
     images = jnp.zeros((div.shape[0], span), f32)
 
+    def place_of(x, y):
+        chip = 4 * x + y
+        q = jnp.int32(12)
+        for k, (a, b) in enumerate(OWNERS):
+            q = jnp.where(chip == 4 * a + b, k, q)
+        return q
+
     for k in (3, 2, 1, 0):
         mine = solver & (r == k) & (c == k)
 
@@ -326,8 +370,10 @@
                 for j in range(3, k, -1):
                     arrived(prod_in.at[j], PROD_R + j)
                     t = t - prod_in[j]
-                pulled[k] = product(t, whi[...], wlo[...])
-                spread(k, mine, pulled, P_S, P_R, [(k, j) for j in range(k - 1, -1, -1)])
+                pulled[k] = lower(t, whi, wlo, order)
+                spread((k, k), k, mine, pulled, P_S, P_R, [(k, j) for j in range(k - 1, -1, -1)])
+                if k > 0:
+                    give_inverse(k)
 
         @pl.when(jnp.logical_not(mine))
         def _():
@@ -355,6 +401,7 @@
             @pl.when(first)
             def _():
                 invert()
+                give_inverse(3)
 
         at = slice(k * width, (k + 1) * width)
         images = images + product(pulled[k], khi[at, :], klo[at, :])
@@ -364,9 +411,8 @@
     for i, (a, b) in enumerate(offsets):
         x = lax.rem(r + a, 4)
         y = lax.rem(c + b, 4)
-        gap = lax.rem(y - x + 4, 4)
-        owned = gap != 2
-        chunk = 3 * x + jnp.where(gap == 3, 2, gap)
+        chunk = place_of(x, y)
+        owned = chunk < 12
         slot = 2 * i + core
 
         @pl.when(owned)
@@ -393,9 +439,10 @@
             def _():
                 send(away, lambda chunk=chunk: nsend.at[chunk], lambda: nred.at[30], N_S + i, N_R, (2 * z + 1, x, y))
 
-    gap = lax.rem(c - r + 4, 4)
-    owner = solver & (gap != 2)
-    part = jnp.where(gap == 3, 2, gap)
+    place_here = place_of(r, c)
+    owner = solver & (place_here < 12)
+    at_low = solver & (r == LOW[0]) & (c == LOW[1])
+    at_high = solver & (r == HIGH[0]) & (c == HIGH[1])
 
     if relay:
 
@@ -421,68 +468,104 @@
                 Z_R,
                 (2 * lax.rem(z + d, planes) + 1, r, c),
             )
+
+    @pl.when(at_low | at_high)
+    def _():
+        for k in range(2):
+            for i in range(3):
+                for j in range(i + 1):
+                    si = slice(i * order, (i + 1) * order)
+                    sj = slice(j * order, (j + 1) * order)
+                    if j == 0:
+                        at = (k, si, slice(0, (i + 1) * order))
+                        arrived(aux.at[at], BULK_R + 3 * k + i)
+                    dhi[k, sj, si], dlo[k, sj, si] = split2(aux[k, si, sj].T)
+
+    @pl.when(owner)
+    def _():
         arrived(zred.at[0 : planes - 1], Z_R)
         total = zred[0]
         for s in range(1, planes):
             total = total + zred[s]
         mout[...] = total * (1.0 / total_rows)
 
-    passing = owner & (gap != 0)
+    passing = owner & jnp.logical_not(at_low | at_high)
+    goal_low = place_here < 6
+    part = jnp.where(goal_low, place_here, place_here - 6)
 
     @pl.when(passing)
     def _():
-        send(passing, lambda: mout, lambda: min_.at[part], M_S, M_R + part, (dp, r, r))
-
-    @pl.when(diagonal)
-    def _():
-        min_[0] = mout[...]
-        arrived(min_.at[1], M_R + 1)
-        arrived(min_.at[2], M_R + 2)
+        goal = (dp, jnp.where(goal_low, LOW[0], HIGH[0]), jnp.where(goal_low, LOW[1], HIGH[1]))
+        send(passing, lambda: mout, lambda: min_.at[part], M_S, M_R + part, goal)
+
+    def normal(k):
+        base = 3 * (k % 2)
+        for j in range(base, base + 3):
+            if j == 0:
+                min_[0] = mout[...]
+            else:
+                arrived(min_.at[j], M_R + j)
+        joined = jnp.concatenate([min_[base], min_[base + 1], min_[base + 2]], axis=1)
+        return joined + ridge_weight * pulled[k]
+
+    @pl.when(at_low)
+    def _():
+        img[0] = upper(normal(0), dhi.at[0], dlo.at[0], order)
+        spread(LOW, 0, at_low, img, IMG_S, IMG_R, [(2, 0), (3, 0)], 0, 2)
+        t = normal(1) - product(img[0], thi[...], tlo[...])
+        img[1] = upper(t, dhi.at[1], dlo.at[1], order)
+        spread(LOW, 1, at_low, img, IMG_S + 15, IMG_R, [(2, 1), (3, 1)], 0, 2)
+        spread(LOW, 0, at_low, img, IMG_S, IMG_R, [(2, 0), (3, 0)], 2, 15)
+        spread(LOW, 1, at_low, img, IMG_S + 15, IMG_R, [(2, 1), (3, 1)], 2, 15)
+
+    for k in range(2):
+        multiply = solver & (c == k) & (r >= 2)
+
+        @pl.when(multiply)
+        def _():
+            arrived(img.at[k], IMG_R + k)
+            back_out[...] = product(img[k], thi[...], tlo[...])
+            at = 2 * (r - 2) + k
+            send(multiply, lambda: back_out, lambda at=at: back_in.at[at], BACK_S, BACK_R + at, (dp,) + HIGH)
+
+    @pl.when(at_high)
+    def _():
+        for k in (2, 3):
+            t = normal(k)
+            if k == 3:
+                t = t - product(img[2], thi[...], tlo[...])
+            for j in range(2):
+                at = 2 * (k - 2) + j
+                arrived(back_in.at[at], BACK_R + at)
+                t = t - back_in[at]
+            img[k] = upper(t, dhi.at[k - 2], dlo.at[k - 2], order)
+            spread(HIGH, k, at_high, img, IMG_S + 15 * (k - 2), IMG_R, [])
 
     for k in range(4):
-        mine = solver & (r == k) & (c == k)
-
-        @pl.when(mine)
-        def _():
-            t = jnp.concatenate([min_[0], min_[1], min_[2]], axis=1) + ridge_weight * pulled[k]
-            for j in range(k):
-                arrived(back_in.at[j], BACK_R + j)
-                t = t - back_in[j]
-            img[k] = product(t, thi[...], tlo[...])
-            spread(k, mine, img, IMG_S, IMG_R, [(j, k) for j in range(k + 1, 4)])
-
-        @pl.when(jnp.logical_not(mine))
+        known = at_low | (solver & (c == k) & (r >= 2)) if k < 2 else at_high
+
+        @pl.when(jnp.logical_not(known))
         def _():
             arrived(img.at[k], IMG_R + k)
 
-        multiply = solver & (c == k) & (r > k)
-
-        if k < 3:
-
-            @pl.when(multiply)
-            def _():
-                back_out[...] = product(img[k], thi[...], tlo[...])
-                send(multiply, lambda: back_out, lambda: back_in.at[k], BACK_S, BACK_R + k, (dp, r, r))
-
         @pl.when(solver)
         def _():
             give_core0(solver, img, k, IMGF_S, IMG_R)
 
     load_res.wait()
-    load_it.wait()
     gamma = jnp.sum(rev[...] * rev[...], axis=1, keepdims=True)
     segs = [slice(k * width, (k + 1) * width) for k in range(4)]
     curvature = jnp.zeros((rhs, 1), f32)
     for k in range(4):
+        image[:, segs[k]] = img[k]
         curvature += jnp.sum(div[:, segs[k]] * img[k], axis=1, keepdims=True)
     alpha = gamma / curvature
     gamma_next = jnp.zeros((rhs, 1), f32)
     for k in range(4):
         res = rev[:, segs[k]] - alpha * img[k]
-        new_residual[:, segs[k]] = res
         gamma_next += jnp.sum(res * res, axis=1, keepdims=True)
-    new_iterate[...] = itv[...] + alpha * div[...]
-    new_direction[...] = new_residual[...] + (gamma_next / gamma) * div[...]
+    alphas[...] = jnp.broadcast_to(alpha, alphas.shape)
+    betas[...] = jnp.broadcast_to(gamma_next / gamma, betas.shape)
 
     for cond, src, ss in pending:
 
@@ -502,10 +585,10 @@
     vmem = pltpu.VMEM
     hbm = pl.BlockSpec(memory_space=pl.ANY)
     square = (width, width)
-    return pl.pallas_call(
+    image, alphas, betas = pl.pallas_call(
         functools.partial(kernel, planes, total_rows),
         out_shape=(whole, whole, whole),
-        in_specs=[hbm, hbm, pl.BlockSpec(memory_space=pltpu.SMEM)] + [hbm] * 5,
+        in_specs=[hbm, hbm, pl.BlockSpec(memory_space=pltpu.SMEM)] + [hbm] * 4,
         out_specs=(pl.BlockSpec(memory_space=pltpu.VMEM),) * 3,
         scratch_shapes=[
             vmem(square, f32),
@@ -520,7 +603,6 @@
             vmem((total, span), bf16),
             vmem((rhs, total), f32),
             vmem((rhs, total), f32),
-            vmem((rhs, total), f32),
             vmem((4, rhs, width), f32),
             vmem((rhs, width), f32),
             vmem((4, rhs, width), f32),
@@ -528,17 +610,24 @@
             vmem((32, rhs, order), f32),
             vmem((planes, rhs, order), f32),
             vmem((rhs, order), f32),
-            vmem((3, rhs, order), f32),
+            vmem((6, rhs, order), f32),
             vmem((4, rhs, width), f32),
             vmem((rhs, width), f32),
             vmem((4, rhs, width), f32),
+            vmem((2,) + square, f32),
+            vmem((2,) + square, bf16),
+            vmem((2,) + square, bf16),
             pltpu.SemaphoreType.DMA((S.count,)),
             pltpu.SemaphoreType.REGULAR,
         ],
         compiler_params=pltpu.CompilerParams(
-            collective_id=0, has_side_effects=True, vmem_limit_bytes=50 * 1024 * 1024
+            collective_id=0, has_side_effects=True, vmem_limit_bytes=64 * 1024 * 1024 - 65536
         ),
-    )(data, centres, scales, factor, block_inv, iterate, residual, direction)
+    )(data, centres, scales, factor, block_inv, residual, direction)
+    new_iterate = iterate + alphas * direction
+    new_residual = residual - alphas * image
+    new_direction = new_residual + betas * direction
+    return new_iterate, new_residual, new_direction
 
 
 def solution(mesh):

time: 82.3 us -> 74.4 us (0.904)
  local copies, waits for them, and re-layouts: 9.75 us -> 0 us
  other arithmetic: 0 us -> 1.86 us
    unnamed x19 -> x0, local copies, waits for them, and re-layouts: 9.75 us -> none
    add x0 -> x1, other arithmetic: none -> 1.86 us  [per_device(): new_direction = new_residual + betas * direction]
where the time goes in v2:
time: 74.4 us; the launch traced here: 74.2 us
  Pallas kernels  71.7 us (96%)
  other arithmetic  1.86 us (2%)
    pallas_call x1, Pallas kernels, per_device(): pl.pallas_call(functools.partial(kernel, planes, total_rows), out_shape=(...  71.7 us
    add x1, other arithmetic, per_device(): new_direction = new_residual + betas * direction  1.86 us

profile of v2, /device:TPU:1, one launch (start us, length us, event | category | flops | bytes accessed | tf_op | source)
XLA Modules:
  0.0 74.2 jit_solution(1594831799612089470)
XLA Ops:
  0.6 71.7 %shard_map.103 = (f32[8,3072]{1,0:T(8,128)}, f32[8,3072]{1,0:T(8,128)}, f32[8,3072]{1,0:T(8,128)}) custom-call(f32[16,2048]{1,0:T(8,128)} %data.1, f32[16,768]{1,0:T(8,128)} %centres.1, f32[16]{0:T(128)} %scales.1, f32[768,768]{1,0:T(8,128)} %factor.1, f32[3,256,256]{2,1,0:T(8,128)} %block_inv.1, f32[8,3072]{1,0:T(8,128)} %residual.1, f32[8,3072]{1,0:T(8,128)} %direction.1), custom_call_target="tpu_custom_call" | custom-call | tf_op jit(solution)/shard_map/pallas_call | solution.py:588
  72.4 1.9 %multiply_add_fusion = (f32[8,3072]{1,0:T(8,128)}, f32[8,3072]{1,0:T(8,128)}, f32[8,3072]{1,0:T(8,128)}) fusion(f32[8,3072]{1,0:T(8,128)} %get-tuple-element.8, f32[8,3072]{1,0:T(8,128)} %direction.1, f32[8,3072]{1,0:T(8,128)} %residual.1, f32[8,3072]{1,0:T(8,128)} %get-tuple-element.6, f32[8,3072]{1,0:T(8,128)} %get-tuple-element.7, f32[8,3072]{1,0:T(8,128)} %param.13), kind=kLoop, calls=%fused_computation | loop fusion | flops 147456 | bytes 884736 | tf_op jit(solution)/shard_map/add | solution.py:629

commit v3 on v2

--- a/solution.py
+++ b/solution.py
@@ -95,6 +95,7 @@
 BACK_S = S.take(1)
 BULK_R = S.take(6)
 BULK_S = S.take(3)
+LEAD_S = S.take(16)
 
 
 def kernel(
@@ -178,9 +179,12 @@
     load_res = local(residual, rev, 5)
     diagonal = solver & (r == c)
     below = solver & (r > c)
+    at_low = solver & (r == LOW[0]) & (c == LOW[1])
+    at_high = solver & (r == HIGH[0]) & (c == HIGH[1])
+    lead = z == 0
     holders = [solver & (r == k) & (c == k) for k in range(4)]
 
-    @pl.when(diagonal)
+    @pl.when(diagonal | at_low | at_high)
     def _():
         load_inv.start()
 
@@ -195,8 +199,7 @@
     load_res.start()
 
     barrier = pltpu.get_barrier_semaphore()
-    near = sorted({d % planes for d in (1, 2, 3, 4, -1, -2, -3, -4)} - {0})
-    relay = sorted({d % planes for d in (4, -4)}) if planes > 9 else []
+    far = sorted(range(1, planes), key=lambda d: -ring_distance(d, planes))
     offsets = sorted(
         [(a, b) for a in range(4) for b in range(4)],
         key=lambda o: (-ring_distance(o[0], 4) - ring_distance(o[1], 4), o),
@@ -209,8 +212,8 @@
     def _():
         for a, b in offsets[:-1]:
             signal(barrier, (dp, lax.rem(r + a, 4), lax.rem(c + b, 4)))
-        for d in near:
-            signal(barrier, (2 * lax.rem(z + d, planes) + 1, r, c))
+        for d in far:
+            signal(barrier, (2 * lax.rem(z + d, planes), r, c))
         signal(barrier, (dp - 1, r, c))
 
     @pl.when(core == 0)
@@ -219,7 +222,7 @@
 
     load_dir.wait()
 
-    first = solver & (r == 3) & (c == 3)
+    first = holders[3] & lead
 
     @pl.when(first)
     def _():
@@ -242,58 +245,6 @@
         whi[si, sj], wlo[si, sj] = split2(v)
         thi[sj, si], tlo[sj, si] = split2(v.T)
 
-    @pl.when(below)
-    def _():
-        load_fac.wait()
-        for i in range(3):
-            for j in range(3):
-                keep(fac[i * order : (i + 1) * order, j * order : (j + 1) * order], i, j)
-
-    @pl.when(solver)
-    def _():
-        pl.semaphore_wait(barrier, 15 + len(near) + 1)
-        for d in relay:
-            signal(zready, (2 * lax.rem(z + d, planes) + 1, r, c))
-
-    @pl.when(core == 0)
-    def _():
-        pl.semaphore_wait(barrier, 1)
-
-    def spread(source, k, cond, buf, ss, rs, urgent, first=0, last=15):
-        goals = [((source[0] + a) % 4, (source[1] + b) % 4) for a, b in offsets[:-1]]
-        goals = urgent + [g for g in goals if g not in urgent]
-        for i, (a, b) in enumerate(goals):
-            if first <= i < last:
-                send(cond, lambda: buf.at[k], lambda: buf.at[k], ss + i, rs + k, (dp, a, b))
-
-    def give_inverse(k):
-        cond = holders[k]
-        goal = LOW if k < 2 else HIGH
-        for i in range(3):
-            at = (slice(i * order, (i + 1) * order), slice(0, (i + 1) * order))
-            send(
-                cond,
-                lambda at=at: fac.at[at],
-                lambda: aux.at[(k % 2,) + at],
-                BULK_S + i,
-                BULK_R + 3 * (k % 2) + i,
-                (dp,) + goal,
-            )
-
-    def give_core0(cond, buf, k, ss, rs):
-        send(cond, lambda: buf.at[k], lambda: buf.at[k], ss + k, rs + k, (dp - 1, r, c))
-
-    @pl.when(first)
-    def _():
-        spread((3, 3), 3, first, pulled, P_S, P_R, [(3, 2), (3, 1), (3, 0)])
-
-    load_cen.wait()
-
-    @pl.when(solver)
-    def _():
-        for i, d in enumerate((2, 1, 3)):
-            send(solver, lambda: cen.at[c], lambda: cen.at[c], CEN_S + i, CEN_R + c, (dp, r, lax.rem(c + d, 4)))
-
     def invert():
         b = [slice(k * order, (k + 1) * order) for k in range(3)]
         mul = functools.partial(dot, precision=HIGHEST)
@@ -306,15 +257,68 @@
                 fac[b[i], b[j]] = v
                 whi[b[i], b[j]], wlo[b[i], b[j]] = split2(v)
 
-    @pl.when(diagonal & (r != 3))
+    @pl.when(diagonal & jnp.logical_not(first))
     def _():
         load_inv.wait()
         load_fac.wait()
         invert()
 
-    @pl.when(diagonal & (r == 0))
-    def _():
-        give_inverse(0)
+    @pl.when(below)
+    def _():
+        load_fac.wait()
+        for i in range(3):
+            for j in range(3):
+                keep(fac[i * order : (i + 1) * order, j * order : (j + 1) * order], i, j)
+
+    @pl.when(solver)
+    def _():
+        pl.semaphore_wait(barrier, 16)
+
+    @pl.when(core == 0)
+    def _():
+        pl.semaphore_wait(barrier, planes)
+        signal(zready, (dp + 1, r, c))
+
+    def spread(source, k, cond, buf, ss, rs, urgent, first=0, last=15):
+        goals = [((source[0] + a) % 4, (source[1] + b) % 4) for a, b in offsets[:-1]]
+        goals = urgent + [g for g in goals if g not in urgent]
+        for i, (a, b) in enumerate(goals):
+            if first <= i < last:
+                send(cond, lambda: buf.at[k], lambda: buf.at[k], ss + i, rs + k, (dp, a, b))
+
+    def give_inverse(k, cond):
+        goal = LOW if k < 2 else HIGH
+        for i in range(k % 2, 3):
+            at = (slice(i * order, (i + 1) * order), slice(0, (i + 1 - k % 2) * order))
+            send(
+                cond,
+                lambda at=at: fac.at[at],
+                lambda: aux.at[(k % 2,) + at],
+                BULK_S + i,
+                BULK_R + 3 * (k % 2) + i,
+                (dp,) + goal,
+            )
+
+    def give_core0(cond, buf, k, ss, rs):
+        send(cond, lambda: buf.at[k], lambda: buf.at[k], ss + k, rs + k, (dp - 1, r, c))
+
+    @pl.when(first)
+    def _():
+        spread((3, 3), 3, first, pulled, P_S, P_R, [(3, 2), (3, 1), (3, 0)])
+
+    load_cen.wait()
+
+    @pl.when(solver)
+    def _():
+        for i, d in enumerate((2, 1, 3)):
+            send(solver, lambda: cen.at[c], lambda: cen.at[c], CEN_S + i, CEN_R + c, (dp, r, lax.rem(c + d, 4)))
+
+    for k in range(4):
+        early = holders[k] if k == 0 else holders[k] & jnp.logical_not(lead)
+
+        @pl.when(early)
+        def _():
+            give_inverse(k, early)
 
     scale_col = jnp.zeros((rows.shape[0], 1), f32)
     place = lax.broadcasted_iota(jnp.int32, (rows.shape[0], 1), 0)
@@ -346,7 +350,9 @@
                 at = slice(k * width + q * order, k * width + (q + 1) * order)
                 khi[at, :], klo[at, :] = split2(v)
 
-    @pl.when((r != 3) | (core == 0))
+    late = solver & (r == 3) & lead
+
+    @pl.when(jnp.logical_not(late))
     def _():
         tiles()
 
@@ -360,26 +366,34 @@
         return q
 
     for k in (3, 2, 1, 0):
-        mine = solver & (r == k) & (c == k)
+        mine = holders[k]
+        leading = mine & lead
+        led = mine & jnp.logical_not(lead)
+        nearby = [(k, j) for j in range(k - 1, -1, -1)]
 
         if k < 3:
 
-            @pl.when(mine)
+            @pl.when(leading)
             def _():
                 t = div[:, k * width : (k + 1) * width]
                 for j in range(3, k, -1):
                     arrived(prod_in.at[j], PROD_R + j)
                     t = t - prod_in[j]
                 pulled[k] = lower(t, whi, wlo, order)
-                spread((k, k), k, mine, pulled, P_S, P_R, [(k, j) for j in range(k - 1, -1, -1)])
+                spread((k, k), k, leading, pulled, P_S, P_R, nearby)
                 if k > 0:
-                    give_inverse(k)
+                    give_inverse(k, leading)
+
+        @pl.when(led)
+        def _():
+            arrived(pulled.at[k], P_R + k)
+            spread((k, k), k, led, pulled, P_S, P_R, [])
 
         @pl.when(jnp.logical_not(mine))
         def _():
             arrived(pulled.at[k], P_R + k)
 
-        multiply = solver & (r == k) & (c < k)
+        multiply = solver & lead & (r == k) & (c < k)
 
         if k > 0:
 
@@ -394,14 +408,21 @@
 
         if k == 3:
 
-            @pl.when((r == 3) & solver)
+            @pl.when(late)
             def _():
                 tiles()
 
             @pl.when(first)
             def _():
                 invert()
-                give_inverse(3)
+                give_inverse(3, first)
+
+        @pl.when(leading)
+        def _():
+            pl.semaphore_wait(zready, 1)
+            for i, d in enumerate(far):
+                goal = (2 * lax.rem(z + d, planes) + 1, k, k)
+                send(leading, lambda: pulled.at[k], lambda: pulled.at[k], LEAD_S + i, P_R + k, goal)
 
         at = slice(k * width, (k + 1) * width)
         images = images + product(pulled[k], khi[at, :], klo[at, :])
@@ -441,16 +462,10 @@
 
     place_here = place_of(r, c)
     owner = solver & (place_here < 12)
-    at_low = solver & (r == LOW[0]) & (c == LOW[1])
-    at_high = solver & (r == HIGH[0]) & (c == HIGH[1])
-
-    if relay:
-
-        @pl.when(solver)
-        def _():
-            pl.semaphore_wait(zready, len(relay))
-
-    far = sorted(range(1, planes), key=lambda d: -ring_distance(d, planes))
+
+    @pl.when(solver & jnp.logical_not(diagonal & lead))
+    def _():
+        pl.semaphore_wait(zready, 1)
 
     @pl.when(owner)
     def _():
@@ -471,15 +486,17 @@
 
     @pl.when(at_low | at_high)
     def _():
+        load_inv.wait()
         for k in range(2):
             for i in range(3):
                 for j in range(i + 1):
                     si = slice(i * order, (i + 1) * order)
                     sj = slice(j * order, (j + 1) * order)
-                    if j == 0:
-                        at = (k, si, slice(0, (i + 1) * order))
+                    if j == 0 and i >= k:
+                        at = (k, si, slice(0, (i + 1 - k) * order))
                         arrived(aux.at[at], BULK_R + 3 * k + i)
-                    dhi[k, sj, si], dlo[k, sj, si] = split2(aux[k, si, sj].T)
+                    block = inv[i] if i == j and k == 1 else aux[k, si, sj]
+                    dhi[k, sj, si], dlo[k, sj, si] = split2(block.T)
 
     @pl.when(owner)
     def _():

time: 74.4 us -> 75.9 us (1.020)
  Pallas kernels: 71.7 us -> 73.2 us
    pallas_call x1, Pallas kernels: 71.7 us -> 73.2 us  [per_device(): pl.pallas_call(functools.partial(kernel, planes, total_rows), out_shape=(...]
where the time goes in v3:
time: 75.9 us; the launch traced here: 75.7 us
  Pallas kernels  73.2 us (96%)
  other arithmetic  1.86 us (2%)
    pallas_call x1, Pallas kernels, per_device(): pl.pallas_call(functools.partial(kernel, planes, total_rows), out_shape=(...  73.2 us
    add x1, other arithmetic, per_device(): new_direction = new_residual + betas * direction  1.86 us

profile of v3, /device:TPU:1, one launch (start us, length us, event | category | flops | bytes accessed | tf_op | source)
XLA Modules:
  0.0 75.7 jit_solution(13488344439984345040)
XLA Ops:
  0.6 73.2 %shard_map.103 = (f32[8,3072]{1,0:T(8,128)}, f32[8,3072]{1,0:T(8,128)}, f32[8,3072]{1,0:T(8,128)}) custom-call(f32[16,2048]{1,0:T(8,128)} %data.1, f32[16,768]{1,0:T(8,128)} %centres.1, f32[16]{0:T(128)} %scales.1, f32[768,768]{1,0:T(8,128)} %factor.1, f32[3,256,256]{2,1,0:T(8,128)} %block_inv.1, f32[8,3072]{1,0:T(8,128)} %residual.1, f32[8,3072]{1,0:T(8,128)} %direction.1), custom_call_target="tpu_custom_call" | custom-call | tf_op jit(solution)/shard_map/pallas_call | solution.py:605
  73.8 1.9 %multiply_add_fusion = (f32[8,3072]{1,0:T(8,128)}, f32[8,3072]{1,0:T(8,128)}, f32[8,3072]{1,0:T(8,128)}) fusion(f32[8,3072]{1,0:T(8,128)} %get-tuple-element.8, f32[8,3072]{1,0:T(8,128)} %direction.1, f32[8,3072]{1,0:T(8,128)} %residual.1, f32[8,3072]{1,0:T(8,128)} %get-tuple-element.6, f32[8,3072]{1,0:T(8,128)} %get-tuple-element.7, f32[8,3072]{1,0:T(8,128)} %param.13), kind=kLoop, calls=%fused_computation | loop fusion | flops 147456 | bytes 884736 | tf_op jit(solution)/shard_map/add | solution.py:646

commit v4 on v3

--- a/solution.py
+++ b/solution.py
@@ -69,6 +69,7 @@
 
 
 OWNERS = ((1, 0), (0, 0), (2, 0), (1, 1), (1, 3), (0, 1), (3, 2), (2, 2), (0, 2), (3, 3), (3, 1), (2, 3))
+PLACES = ((1, 0), (2, 0), (2, 1), (0, 0), (1, 1), (2, 2))
 LOW = (1, 0)
 HIGH = (3, 2)
 
@@ -93,9 +94,8 @@
 IMGF_S = S.take(4)
 BACK_R = S.take(4)
 BACK_S = S.take(1)
-BULK_R = S.take(6)
-BULK_S = S.take(3)
-LEAD_S = S.take(16)
+BULK_R = S.take(2)
+BULK_S = S.take(1)
 
 
 def kernel(
@@ -134,6 +134,7 @@
     img,
     back_out,
     back_in,
+    blocks,
     aux,
     dhi,
     dlo,
@@ -171,6 +172,18 @@
         remote(src(), dst(), ss, rs, dev).start()
         pending.append((cond, src, ss))
 
+    def flush():
+        groups = {}
+        for cond, src, ss in pending:
+            groups.setdefault(id(cond), (cond, []))[1].append((src, ss))
+        pending.clear()
+        for cond, sends in groups.values():
+
+            @pl.when(cond)
+            def _():
+                for src, ss in sends:
+                    arrived(src(), ss)
+
     load_fac = local(factor, fac, 0)
     load_inv = local(block_inv, inv, 1)
     load_dir = local(direction, div, 2)
@@ -181,7 +194,6 @@
     below = solver & (r > c)
     at_low = solver & (r == LOW[0]) & (c == LOW[1])
     at_high = solver & (r == HIGH[0]) & (c == HIGH[1])
-    lead = z == 0
     holders = [solver & (r == k) & (c == k) for k in range(4)]
 
     @pl.when(diagonal | at_low | at_high)
@@ -222,7 +234,7 @@
 
     load_dir.wait()
 
-    first = holders[3] & lead
+    first = holders[3]
 
     @pl.when(first)
     def _():
@@ -254,7 +266,7 @@
         x20 = -mul(a2, mul(fac[b[2], b[0]], a0) + mul(fac[b[2], b[1]], x10))
         for i, row in enumerate(((a0,), (x10, a1), (x20, x21, a2))):
             for j, v in enumerate(row):
-                fac[b[i], b[j]] = v
+                blocks[PLACES.index((i, j))] = v
                 whi[b[i], b[j]], wlo[b[i], b[j]] = split2(v)
 
     @pl.when(diagonal & jnp.logical_not(first))
@@ -288,16 +300,9 @@
 
     def give_inverse(k, cond):
         goal = LOW if k < 2 else HIGH
-        for i in range(k % 2, 3):
-            at = (slice(i * order, (i + 1) * order), slice(0, (i + 1 - k % 2) * order))
-            send(
-                cond,
-                lambda at=at: fac.at[at],
-                lambda: aux.at[(k % 2,) + at],
-                BULK_S + i,
-                BULK_R + 3 * (k % 2) + i,
-                (dp,) + goal,
-            )
+        n = 6 - 3 * (k % 2)
+        src = lambda: blocks.at[0:n]
+        send(cond, src, lambda: aux.at[k % 2, 0:n], BULK_S, BULK_R + k % 2, (dp,) + goal)
 
     def give_core0(cond, buf, k, ss, rs):
         send(cond, lambda: buf.at[k], lambda: buf.at[k], ss + k, rs + k, (dp - 1, r, c))
@@ -313,12 +318,11 @@
         for i, d in enumerate((2, 1, 3)):
             send(solver, lambda: cen.at[c], lambda: cen.at[c], CEN_S + i, CEN_R + c, (dp, r, lax.rem(c + d, 4)))
 
-    for k in range(4):
-        early = holders[k] if k == 0 else holders[k] & jnp.logical_not(lead)
-
-        @pl.when(early)
-        def _():
-            give_inverse(k, early)
+    for k in (0, 2):
+
+        @pl.when(holders[k])
+        def _():
+            give_inverse(k, holders[k])
 
     scale_col = jnp.zeros((rows.shape[0], 1), f32)
     place = lax.broadcasted_iota(jnp.int32, (rows.shape[0], 1), 0)
@@ -350,7 +354,7 @@
                 at = slice(k * width + q * order, k * width + (q + 1) * order)
                 khi[at, :], klo[at, :] = split2(v)
 
-    late = solver & (r == 3) & lead
+    late = solver & (r == 3)
 
     @pl.when(jnp.logical_not(late))
     def _():
@@ -367,33 +371,26 @@
 
     for k in (3, 2, 1, 0):
         mine = holders[k]
-        leading = mine & lead
-        led = mine & jnp.logical_not(lead)
         nearby = [(k, j) for j in range(k - 1, -1, -1)]
 
         if k < 3:
 
-            @pl.when(leading)
+            @pl.when(mine)
             def _():
                 t = div[:, k * width : (k + 1) * width]
                 for j in range(3, k, -1):
                     arrived(prod_in.at[j], PROD_R + j)
                     t = t - prod_in[j]
                 pulled[k] = lower(t, whi, wlo, order)
-                spread((k, k), k, leading, pulled, P_S, P_R, nearby)
-                if k > 0:
-                    give_inverse(k, leading)
-
-        @pl.when(led)
+                spread((k, k), k, mine, pulled, P_S, P_R, nearby)
+                if k == 1:
+                    give_inverse(k, mine)
+
+        @pl.when(jnp.logical_not(mine))
         def _():
             arrived(pulled.at[k], P_R + k)
-            spread((k, k), k, led, pulled, P_S, P_R, [])
-
-        @pl.when(jnp.logical_not(mine))
-        def _():
-            arrived(pulled.at[k], P_R + k)
-
-        multiply = solver & lead & (r == k) & (c < k)
+
+        multiply = solver & (r == k) & (c < k)
 
         if k > 0:
 
@@ -416,13 +413,6 @@
             def _():
                 invert()
                 give_inverse(3, first)
-
-        @pl.when(leading)
-        def _():
-            pl.semaphore_wait(zready, 1)
-            for i, d in enumerate(far):
-                goal = (2 * lax.rem(z + d, planes) + 1, k, k)
-                send(leading, lambda: pulled.at[k], lambda: pulled.at[k], LEAD_S + i, P_R + k, goal)
 
         at = slice(k * width, (k + 1) * width)
         images = images + product(pulled[k], khi[at, :], klo[at, :])
@@ -463,7 +453,7 @@
     place_here = place_of(r, c)
     owner = solver & (place_here < 12)
 
-    @pl.when(solver & jnp.logical_not(diagonal & lead))
+    @pl.when(solver)
     def _():
         pl.semaphore_wait(zready, 1)
 
@@ -488,15 +478,14 @@
     def _():
         load_inv.wait()
         for k in range(2):
-            for i in range(3):
-                for j in range(i + 1):
-                    si = slice(i * order, (i + 1) * order)
-                    sj = slice(j * order, (j + 1) * order)
-                    if j == 0 and i >= k:
-                        at = (k, si, slice(0, (i + 1 - k) * order))
-                        arrived(aux.at[at], BULK_R + 3 * k + i)
-                    block = inv[i] if i == j and k == 1 else aux[k, si, sj]
-                    dhi[k, sj, si], dlo[k, sj, si] = split2(block.T)
+            arrived(aux.at[k, 0 : 6 - 3 * k], BULK_R + k)
+            for n, (i, j) in enumerate(PLACES):
+                si = slice(i * order, (i + 1) * order)
+                sj = slice(j * order, (j + 1) * order)
+                block = inv[i] if i == j and k == 1 else aux[k, n]
+                dhi[k, sj, si], dlo[k, sj, si] = split2(block.T)
+
+    flush()
 
     @pl.when(owner)
     def _():
@@ -584,11 +573,7 @@
     alphas[...] = jnp.broadcast_to(alpha, alphas.shape)
     betas[...] = jnp.broadcast_to(gamma_next / gamma, betas.shape)
 
-    for cond, src, ss in pending:
-
-        @pl.when(cond)
-        def _():
-            arrived(src(), ss)
+    flush()
 
 
 def per_device(data, centres, scales, factor, block_inv, iterate, residual, direction):
@@ -631,7 +616,8 @@
             vmem((4, rhs, width), f32),
             vmem((rhs, width), f32),
             vmem((4, rhs, width), f32),
-            vmem((2,) + square, f32),
+            vmem((6, order, order), f32),
+            vmem((2, 6, order, order), f32),
             vmem((2,) + square, bf16),
             vmem((2,) + square, bf16),
             pltpu.SemaphoreType.DMA((S.count,)),

time: 75.9 us -> 76.1 us (level)
  no operation moved by 1% of the time
where the time goes in v4:
time: 76.1 us; the launch traced here: 75.9 us
  Pallas kernels  73.4 us (96%)
  other arithmetic  1.86 us (2%)
    pallas_call x1, Pallas kernels, per_device(): pl.pallas_call(functools.partial(kernel, planes, total_rows), out_shape=(...  73.4 us
    add x1, other arithmetic, per_device(): new_direction = new_residual + betas * direction  1.86 us

profile of v4, /device:TPU:1, one launch (start us, length us, event | category | flops | bytes accessed | tf_op | source)
XLA Modules:
  0.0 75.9 jit_solution(11951016697325446374)
XLA Ops:
  0.6 73.4 %shard_map.103 = (f32[8,3072]{1,0:T(8,128)}, f32[8,3072]{1,0:T(8,128)}, f32[8,3072]{1,0:T(8,128)}) custom-call(f32[16,2048]{1,0:T(8,128)} %data.1, f32[16,768]{1,0:T(8,128)} %centres.1, f32[16]{0:T(128)} %scales.1, f32[768,768]{1,0:T(8,128)} %factor.1, f32[3,256,256]{2,1,0:T(8,128)} %block_inv.1, f32[8,3072]{1,0:T(8,128)} %residual.1, f32[8,3072]{1,0:T(8,128)} %direction.1), custom_call_target="tpu_custom_call" | custom-call | tf_op jit(solution)/shard_map/pallas_call | solution.py:590
  74.0 1.9 %multiply_add_fusion = (f32[8,3072]{1,0:T(8,128)}, f32[8,3072]{1,0:T(8,128)}, f32[8,3072]{1,0:T(8,128)}) fusion(f32[8,3072]{1,0:T(8,128)} %get-tuple-element.8, f32[8,3072]{1,0:T(8,128)} %direction.1, f32[8,3072]{1,0:T(8,128)} %residual.1, f32[8,3072]{1,0:T(8,128)} %get-tuple-element.6, f32[8,3072]{1,0:T(8,128)} %get-tuple-element.7, f32[8,3072]{1,0:T(8,128)} %param.13), kind=kLoop, calls=%fused_computation | loop fusion | flops 147456 | bytes 884736 | tf_op jit(solution)/shard_map/add | solution.py:632

commit v5 on v4

--- a/solution.py
+++ b/solution.py
@@ -194,15 +194,16 @@
     below = solver & (r > c)
     at_low = solver & (r == LOW[0]) & (c == LOW[1])
     at_high = solver & (r == HIGH[0]) & (c == HIGH[1])
+    helpers = [(core == 0) & (r == k) & (c == k) for k in range(4)]
     holders = [solver & (r == k) & (c == k) for k in range(4)]
 
-    @pl.when(diagonal | at_low | at_high)
+    @pl.when((r == c) | at_low | at_high)
     def _():
         load_inv.start()
 
     load_dir.start()
 
-    @pl.when(diagonal | below)
+    @pl.when((r == c) | below)
     def _():
         load_fac.start()
 
@@ -227,6 +228,13 @@
         for d in far:
             signal(barrier, (2 * lax.rem(z + d, planes), r, c))
         signal(barrier, (dp - 1, r, c))
+
+    for here, users in ((at_low, (0, 1)), (at_high, (2, 3))):
+
+        @pl.when(here)
+        def _():
+            for k in users:
+                signal(barrier, (dp - 1, k, k))
 
     @pl.when(core == 0)
     def _():
@@ -269,7 +277,7 @@
                 blocks[PLACES.index((i, j))] = v
                 whi[b[i], b[j]], wlo[b[i], b[j]] = split2(v)
 
-    @pl.when(diagonal & jnp.logical_not(first))
+    @pl.when((r == c) & jnp.logical_not(first))
     def _():
         load_inv.wait()
         load_fac.wait()
@@ -288,7 +296,7 @@
 
     @pl.when(core == 0)
     def _():
-        pl.semaphore_wait(barrier, planes)
+        pl.semaphore_wait(barrier, planes + jnp.where(r == c, 1, 0))
         signal(zready, (dp + 1, r, c))
 
     def spread(source, k, cond, buf, ss, rs, urgent, first=0, last=15):
@@ -302,7 +310,7 @@
         goal = LOW if k < 2 else HIGH
         n = 6 - 3 * (k % 2)
         src = lambda: blocks.at[0:n]
-        send(cond, src, lambda: aux.at[k % 2, 0:n], BULK_S, BULK_R + k % 2, (dp,) + goal)
+        send(cond, src, lambda: aux.at[k % 2, 0:n], BULK_S, BULK_R + k % 2, (dp + 1,) + goal)
 
     def give_core0(cond, buf, k, ss, rs):
         send(cond, lambda: buf.at[k], lambda: buf.at[k], ss + k, rs + k, (dp - 1, r, c))
@@ -318,11 +326,11 @@
         for i, d in enumerate((2, 1, 3)):
             send(solver, lambda: cen.at[c], lambda: cen.at[c], CEN_S + i, CEN_R + c, (dp, r, lax.rem(c + d, 4)))
 
-    for k in (0, 2):
-
-        @pl.when(holders[k])
-        def _():
-            give_inverse(k, holders[k])
+    for k in range(4):
+
+        @pl.when(helpers[k])
+        def _():
+            give_inverse(k, helpers[k])
 
     scale_col = jnp.zeros((rows.shape[0], 1), f32)
     place = lax.broadcasted_iota(jnp.int32, (rows.shape[0], 1), 0)
@@ -383,8 +391,6 @@
                     t = t - prod_in[j]
                 pulled[k] = lower(t, whi, wlo, order)
                 spread((k, k), k, mine, pulled, P_S, P_R, nearby)
-                if k == 1:
-                    give_inverse(k, mine)
 
         @pl.when(jnp.logical_not(mine))
         def _():
@@ -408,11 +414,6 @@
             @pl.when(late)
             def _():
                 tiles()
-
-            @pl.when(first)
-            def _():
-                invert()
-                give_inverse(3, first)
 
         at = slice(k * width, (k + 1) * width)
         images = images + product(pulled[k], khi[at, :], klo[at, :])

time: 76.1 us -> 69.7 us (0.916)
  Pallas kernels: 73.4 us -> 67 us
    pallas_call x1, Pallas kernels: 73.4 us -> 67 us  [per_device(): pl.pallas_call(functools.partial(kernel, planes, total_rows), out_shape=(...]
where the time goes in v5:
time: 69.7 us; the launch traced here: 69.5 us
  Pallas kernels  67 us (96%)
  other arithmetic  1.86 us (3%)
    pallas_call x1, Pallas kernels, per_device(): pl.pallas_call(functools.partial(kernel, planes, total_rows), out_shape=(...  67 us
    add x1, other arithmetic, per_device(): new_direction = new_residual + betas * direction  1.86 us

profile of v5, /device:TPU:1, one launch (start us, length us, event | category | flops | bytes accessed | tf_op | source)
XLA Modules:
  0.0 69.5 jit_solution(14742482878719024138)
XLA Ops:
  0.6 67.0 %shard_map.103 = (f32[8,3072]{1,0:T(8,128)}, f32[8,3072]{1,0:T(8,128)}, f32[8,3072]{1,0:T(8,128)}) custom-call(f32[16,2048]{1,0:T(8,128)} %data.1, f32[16,768]{1,0:T(8,128)} %centres.1, f32[16]{0:T(128)} %scales.1, f32[768,768]{1,0:T(8,128)} %factor.1, f32[3,256,256]{2,1,0:T(8,128)} %block_inv.1, f32[8,3072]{1,0:T(8,128)} %residual.1, f32[8,3072]{1,0:T(8,128)} %direction.1), custom_call_target="tpu_custom_call" | custom-call | tf_op jit(solution)/shard_map/pallas_call | solution.py:591
  67.7 1.9 %multiply_add_fusion = (f32[8,3072]{1,0:T(8,128)}, f32[8,3072]{1,0:T(8,128)}, f32[8,3072]{1,0:T(8,128)}) fusion(f32[8,3072]{1,0:T(8,128)} %get-tuple-element.8, f32[8,3072]{1,0:T(8,128)} %direction.1, f32[8,3072]{1,0:T(8,128)} %residual.1, f32[8,3072]{1,0:T(8,128)} %get-tuple-element.6, f32[8,3072]{1,0:T(8,128)} %get-tuple-element.7, f32[8,3072]{1,0:T(8,128)} %param.13), kind=kLoop, calls=%fused_computation | loop fusion | flops 147456 | bytes 884736 | tf_op jit(solution)/shard_map/add | solution.py:633

commit v6 on v5

--- a/solution.py
+++ b/solution.py
@@ -81,8 +81,10 @@
 P_R = S.take(4)
 P_S = S.take(16)
 PF_S = S.take(4)
-PROD_R = S.take(4)
-PROD_S = S.take(1)
+PROD_R = S.take(12)
+PROD_S = S.take(3)
+PIECE_R = S.take(3)
+PIECE_S = S.take(6)
 N_R = S.take(1)
 N_S = S.take(16)
 Z_R = S.take(1)
@@ -92,8 +94,8 @@
 IMG_R = S.take(4)
 IMG_S = S.take(30)
 IMGF_S = S.take(4)
-BACK_R = S.take(4)
-BACK_S = S.take(1)
+BACK_R = S.take(12)
+BACK_S = S.take(3)
 BULK_R = S.take(2)
 BULK_S = S.take(1)
 
@@ -299,12 +301,24 @@
         pl.semaphore_wait(barrier, planes + jnp.where(r == c, 1, 0))
         signal(zready, (dp + 1, r, c))
 
-    def spread(source, k, cond, buf, ss, rs, urgent, first=0, last=15):
+    def spread(source, k, cond, buf, ss, rs, urgent, first=0, last=15, skip=()):
         goals = [((source[0] + a) % 4, (source[1] + b) % 4) for a, b in offsets[:-1]]
         goals = urgent + [g for g in goals if g not in urgent]
         for i, (a, b) in enumerate(goals):
-            if first <= i < last:
+            if first <= i < last and (a, b) not in skip:
                 send(cond, lambda: buf.at[k], lambda: buf.at[k], ss + i, rs + k, (dp, a, b))
+
+    cut = [slice(i * order, (i + 1) * order) for i in range(3)]
+
+    def pieces_product(take, emit, high, low, sequence):
+        total = None
+        for i in sequence[:2]:
+            term = product(take(i), high[cut[i], :], low[cut[i], :])
+            total = term if total is None else total + term
+        i = sequence[2]
+        v = take(i)
+        for j in sequence:
+            emit(j, total[:, cut[j]] + product(v, high[cut[i], cut[j]], low[cut[i], cut[j]]))
 
     def give_inverse(k, cond):
         goal = LOW if k < 2 else HIGH
@@ -385,25 +399,56 @@
 
             @pl.when(mine)
             def _():
-                t = div[:, k * width : (k + 1) * width]
+                t = [div[:, k * width + i * order : k * width + (i + 1) * order] for i in range(3)]
                 for j in range(3, k, -1):
-                    arrived(prod_in.at[j], PROD_R + j)
-                    t = t - prod_in[j]
-                pulled[k] = lower(t, whi, wlo, order)
-                spread((k, k), k, mine, pulled, P_S, P_R, nearby)
-
-        @pl.when(jnp.logical_not(mine))
+                    for i in (2, 1, 0):
+                        if j > k + 1:
+                            arrived(prod_in.at[j, i], PROD_R + 3 * j + i)
+                            t[i] = t[i] - prod_in[j, i]
+                for i in (2, 1, 0):
+                    arrived(prod_in.at[k + 1, i], PROD_R + 3 * (k + 1) + i)
+                    t[i] = t[i] - prod_in[k + 1, i]
+                    v = jnp.concatenate(t[i:], axis=1)
+                    pulled[k, :, cut[i]] = product(v, whi[i * order :, cut[i]], wlo[i * order :, cut[i]])
+                    if k > 0:
+                        piece = lambda i=i: pulled.at[k, :, cut[i]]
+                        send(mine, piece, piece, PIECE_S + i, PIECE_R + i, (dp, k, k - 1))
+                spread((k, k), k, mine, pulled, P_S, P_R, nearby, skip=nearby[:1])
+
+        multiply = solver & (r == k) & (c < k)
+        pieced = solver & (r == k) & (c == k - 1) if k in (1, 2) else None
+        whole = multiply if pieced is None else multiply & (c < k - 1)
+
+        def give_product(cond):
+            def emit(j, v):
+                prod_out[j] = v
+                send(cond, lambda: prod_out.at[j], lambda: prod_in.at[k, j], PROD_S + j, PROD_R + 3 * k + j, (dp, c, c))
+
+            return emit
+
+        if pieced is not None:
+
+            @pl.when(pieced)
+            def _():
+                def take(i):
+                    arrived(pulled.at[k, :, cut[i]], PIECE_R + i)
+                    return pulled[k, :, cut[i]]
+
+                pieces_product(take, give_product(pieced), whi, wlo, (2, 1, 0))
+
+        known = mine if pieced is None else mine | pieced
+
+        @pl.when(jnp.logical_not(known))
         def _():
             arrived(pulled.at[k], P_R + k)
 
-        multiply = solver & (r == k) & (c < k)
-
-        if k > 0:
-
-            @pl.when(multiply)
+        if k > 1:
+
+            @pl.when(whole)
             def _():
-                prod_out[...] = product(pulled[k], whi[...], wlo[...])
-                send(multiply, lambda: prod_out, lambda: prod_in.at[k], PROD_S, PROD_R + k, (dp, c, c))
+                emit = give_product(whole)
+                for j in (2, 1, 0):
+                    emit(j, product(pulled[k], whi[:, cut[j]], wlo[:, cut[j]]))
 
         @pl.when(solver)
         def _():
@@ -520,8 +565,12 @@
         img[0] = upper(normal(0), dhi.at[0], dlo.at[0], order)
         spread(LOW, 0, at_low, img, IMG_S, IMG_R, [(2, 0), (3, 0)], 0, 2)
         t = normal(1) - product(img[0], thi[...], tlo[...])
-        img[1] = upper(t, dhi.at[1], dlo.at[1], order)
-        spread(LOW, 1, at_low, img, IMG_S + 15, IMG_R, [(2, 1), (3, 1)], 0, 2)
+        for i in range(3):
+            end = (i + 1) * order
+            img[1, :, cut[i]] = product(t[:, :end], dhi[1, :end, cut[i]], dlo[1, :end, cut[i]])
+            piece = lambda i=i: img.at[1, :, cut[i]]
+            for n in range(2):
+                send(at_low, piece, piece, PIECE_S + 3 * n + i, PIECE_R + i, (dp, 2 + n, 1))
         spread(LOW, 0, at_low, img, IMG_S, IMG_R, [(2, 0), (3, 0)], 2, 15)
         spread(LOW, 1, at_low, img, IMG_S + 15, IMG_R, [(2, 1), (3, 1)], 2, 15)
 
@@ -530,10 +579,21 @@
 
         @pl.when(multiply)
         def _():
-            arrived(img.at[k], IMG_R + k)
-            back_out[...] = product(img[k], thi[...], tlo[...])
             at = 2 * (r - 2) + k
-            send(multiply, lambda: back_out, lambda at=at: back_in.at[at], BACK_S, BACK_R + at, (dp,) + HIGH)
+            if k == 0:
+                arrived(img.at[k], IMG_R + k)
+
+            def take(i):
+                if k == 1:
+                    arrived(img.at[k, :, cut[i]], PIECE_R + i)
+                return img[k, :, cut[i]]
+
+            def emit(j, v):
+                back_out[j] = v
+                goal = (dp,) + HIGH
+                send(multiply, lambda: back_out.at[j], lambda: back_in.at[at, j], BACK_S + j, BACK_R + 3 * at + j, goal)
+
+            pieces_product(take, emit, thi, tlo, (0, 1, 2))
 
     @pl.when(at_high)
     def _():
@@ -541,11 +601,16 @@
             t = normal(k)
             if k == 3:
                 t = t - product(img[2], thi[...], tlo[...])
-            for j in range(2):
-                at = 2 * (k - 2) + j
-                arrived(back_in.at[at], BACK_R + at)
-                t = t - back_in[at]
-            img[k] = upper(t, dhi.at[k - 2], dlo.at[k - 2], order)
+            ready = []
+            for i in range(3):
+                part = t[:, cut[i]]
+                for at in (2 * (k - 2), 2 * (k - 2) + 1):
+                    arrived(back_in.at[at, i], BACK_R + 3 * at + i)
+                    part = part - back_in[at, i]
+                ready.append(part)
+                end = (i + 1) * order
+                v = jnp.concatenate(ready, axis=1)
+                img[k, :, cut[i]] = product(v, dhi[k - 2, :end, cut[i]], dlo[k - 2, :end, cut[i]])
             spread(HIGH, k, at_high, img, IMG_S + 15 * (k - 2), IMG_R, [])
 
     for k in range(4):
@@ -607,16 +672,16 @@
             vmem((rhs, total), f32),
             vmem((rhs, total), f32),
             vmem((4, rhs, width), f32),
-            vmem((rhs, width), f32),
-            vmem((4, rhs, width), f32),
+            vmem((3, rhs, order), f32),
+            vmem((4, 3, rhs, order), f32),
             vmem((12, rhs, order), f32),
             vmem((32, rhs, order), f32),
             vmem((planes, rhs, order), f32),
             vmem((rhs, order), f32),
             vmem((6, rhs, order), f32),
             vmem((4, rhs, width), f32),
-            vmem((rhs, width), f32),
-            vmem((4, rhs, width), f32),
+            vmem((3, rhs, order), f32),
+            vmem((4, 3, rhs, order), f32),
             vmem((6, order, order), f32),
             vmem((2, 6, order, order), f32),
             vmem((2,) + square, bf16),

time: 69.7 us -> 70.3 us (level)
  no operation moved by 1% of the time
where the time goes in v6:
time: 70.3 us; the launch traced here: 70.1 us
  Pallas kernels  67.6 us (96%)
  other arithmetic  1.86 us (3%)
    pallas_call x1, Pallas kernels, per_device(): pl.pallas_call(functools.partial(kernel, planes, total_rows), out_shape=(...  67.6 us
    add x1, other arithmetic, per_device(): new_direction = new_residual + betas * direction  1.86 us

profile of v6, /device:TPU:1, one launch (start us, length us, event | category | flops | bytes accessed | tf_op | source)
XLA Modules:
  0.0 70.1 jit_solution(6653233028100309412)
XLA Ops:
  0.6 67.6 %shard_map.103 = (f32[8,3072]{1,0:T(8,128)}, f32[8,3072]{1,0:T(8,128)}, f32[8,3072]{1,0:T(8,128)}) custom-call(f32[16,2048]{1,0:T(8,128)} %data.1, f32[16,768]{1,0:T(8,128)} %centres.1, f32[16]{0:T(128)} %scales.1, f32[768,768]{1,0:T(8,128)} %factor.1, f32[3,256,256]{2,1,0:T(8,128)} %block_inv.1, f32[8,3072]{1,0:T(8,128)} %residual.1, f32[8,3072]{1,0:T(8,128)} %direction.1), custom_call_target="tpu_custom_call" | custom-call | tf_op jit(solution)/shard_map/pallas_call | solution.py:656
  68.2 1.9 %multiply_add_fusion = (f32[8,3072]{1,0:T(8,128)}, f32[8,3072]{1,0:T(8,128)}, f32[8,3072]{1,0:T(8,128)}) fusion(f32[8,3072]{1,0:T(8,128)} %get-tuple-element.8, f32[8,3072]{1,0:T(8,128)} %direction.1, f32[8,3072]{1,0:T(8,128)} %residual.1, f32[8,3072]{1,0:T(8,128)} %get-tuple-element.6, f32[8,3072]{1,0:T(8,128)} %get-tuple-element.7, f32[8,3072]{1,0:T(8,128)} %param.13), kind=kLoop, calls=%fused_computation | loop fusion | flops 147456 | bytes 884736 | tf_op jit(solution)/shard_map/add | solution.py:698

commit v7 on v5

--- a/solution.py
+++ b/solution.py
@@ -185,6 +185,8 @@
                     arrived(src(), ss)
 
     load_fac = local(factor, fac, 0)
+    under = (slice(order, width), slice(0, width - order))
+    load_under = local(factor.at[under], fac.at[under], 6)
     load_inv = local(block_inv, inv, 1)
     load_dir = local(direction, div, 2)
     load_cen = local(centres, cen.at[c], 3)
@@ -203,7 +205,11 @@
 
     load_dir.start()
 
-    @pl.when((r == c) | below)
+    @pl.when(r == c)
+    def _():
+        load_under.start()
+
+    @pl.when(below)
     def _():
         load_fac.start()
 
@@ -223,8 +229,9 @@
 
     @pl.when(solver)
     def _():
-        for a, b in offsets[:-1]:
-            signal(barrier, (dp, lax.rem(r + a, 4), lax.rem(c + b, 4)))
+        for d in (2, 1, 3):
+            signal(barrier, (dp, r, lax.rem(c + d, 4)))
+            signal(barrier, (dp, lax.rem(r + d, 4), c))
         for d in far:
             signal(barrier, (2 * lax.rem(z + d, planes), r, c))
         signal(barrier, (dp - 1, r, c))
@@ -247,7 +254,7 @@
     @pl.when(first)
     def _():
         load_inv.wait()
-        load_fac.wait()
+        load_under.wait()
         b = [slice(k * order, (k + 1) * order) for k in range(3)]
         base = 3 * width
         d = [div[:, base + k * order : base + (k + 1) * order] for k in range(3)]
@@ -280,7 +287,7 @@
     @pl.when((r == c) & jnp.logical_not(first))
     def _():
         load_inv.wait()
-        load_fac.wait()
+        load_under.wait()
         invert()
 
     @pl.when(below)
@@ -292,7 +299,7 @@
 
     @pl.when(solver)
     def _():
-        pl.semaphore_wait(barrier, 16)
+        pl.semaphore_wait(barrier, 7)
 
     @pl.when(core == 0)
     def _():
@@ -317,7 +324,7 @@
 
     @pl.when(first)
     def _():
-        spread((3, 3), 3, first, pulled, P_S, P_R, [(3, 2), (3, 1), (3, 0)])
+        spread((3, 3), 3, first, pulled, P_S, P_R, [(3, 2), (3, 1), (3, 0)], 0, 3)
 
     load_cen.wait()
 
@@ -346,6 +353,10 @@
         @pl.when(solver)
         def _():
             send(solver, lambda src=src: cen.at[src], lambda src=src: cen.at[src], CENF_S + i, CEN_R + src, (dp - 1, r, c))
+
+    @pl.when(first)
+    def _():
+        spread((3, 3), 3, first, pulled, P_S, P_R, [(3, 2), (3, 1), (3, 0)], 3, 15)
 
     def tiles():
         x = rows[...] / scale_col

time: 69.7 us -> 68.9 us (0.989)
  Pallas kernels: 67 us -> 66.2 us
    pallas_call x1, Pallas kernels: 67 us -> 66.2 us  [per_device(): pl.pallas_call(functools.partial(kernel, planes, total_rows), out_shape=(...]
where the time goes in v7:
time: 68.9 us; the launch traced here: 68.7 us
  Pallas kernels  66.2 us (96%)
  other arithmetic  1.86 us (3%)
    pallas_call x1, Pallas kernels, per_device(): pl.pallas_call(functools.partial(kernel, planes, total_rows), out_shape=(...  66.2 us
    add x1, other arithmetic, per_device(): new_direction = new_residual + betas * direction  1.86 us

profile of v7, /device:TPU:1, one launch (start us, length us, event | category | flops | bytes accessed | tf_op | source)
XLA Modules:
  0.0 68.7 jit_solution(3508054568513456424)
XLA Ops:
  0.6 66.2 %shard_map.103 = (f32[8,3072]{1,0:T(8,128)}, f32[8,3072]{1,0:T(8,128)}, f32[8,3072]{1,0:T(8,128)}) custom-call(f32[16,2048]{1,0:T(8,128)} %data.1, f32[16,768]{1,0:T(8,128)} %centres.1, f32[16]{0:T(128)} %scales.1, f32[768,768]{1,0:T(8,128)} %factor.1, f32[3,256,256]{2,1,0:T(8,128)} %block_inv.1, f32[8,3072]{1,0:T(8,128)} %residual.1, f32[8,3072]{1,0:T(8,128)} %direction.1), custom_call_target="tpu_custom_call" | custom-call | tf_op jit(solution)/shard_map/pallas_call | solution.py:602
  66.8 1.9 %multiply_add_fusion = (f32[8,3072]{1,0:T(8,128)}, f32[8,3072]{1,0:T(8,128)}, f32[8,3072]{1,0:T(8,128)}) fusion(f32[8,3072]{1,0:T(8,128)} %get-tuple-element.8, f32[8,3072]{1,0:T(8,128)} %direction.1, f32[8,3072]{1,0:T(8,128)} %residual.1, f32[8,3072]{1,0:T(8,128)} %get-tuple-element.6, f32[8,3072]{1,0:T(8,128)} %get-tuple-element.7, f32[8,3072]{1,0:T(8,128)} %param.13), kind=kLoop, calls=%fused_computation | loop fusion | flops 147456 | bytes 884736 | tf_op jit(solution)/shard_map/add | solution.py:644

commit v8 on v7

--- a/solution.py
+++ b/solution.py
@@ -96,6 +96,7 @@
 BACK_S = S.take(1)
 BULK_R = S.take(2)
 BULK_S = S.take(1)
+BOTH_S = S.take(15)
 
 
 def kernel(
@@ -306,10 +307,12 @@
         pl.semaphore_wait(barrier, planes + jnp.where(r == c, 1, 0))
         signal(zready, (dp + 1, r, c))
 
-    def spread(source, k, cond, buf, ss, rs, urgent, first=0, last=15):
+    def spread(source, k, cond, buf, ss, rs, urgent, first=0, last=15, both=False):
         goals = [((source[0] + a) % 4, (source[1] + b) % 4) for a, b in offsets[:-1]]
         goals = urgent + [g for g in goals if g not in urgent]
         for i, (a, b) in enumerate(goals):
+            if both:
+                send(cond, lambda: buf.at[k], lambda: buf.at[k], BOTH_S + i, rs + k, (dp - 1, a, b))
             if first <= i < last:
                 send(cond, lambda: buf.at[k], lambda: buf.at[k], ss + i, rs + k, (dp, a, b))
 
@@ -401,7 +404,7 @@
                     arrived(prod_in.at[j], PROD_R + j)
                     t = t - prod_in[j]
                 pulled[k] = lower(t, whi, wlo, order)
-                spread((k, k), k, mine, pulled, P_S, P_R, nearby)
+                spread((k, k), k, mine, pulled, P_S, P_R, nearby, both=k == 0)
 
         @pl.when(jnp.logical_not(mine))
         def _():
@@ -416,9 +419,11 @@
                 prod_out[...] = product(pulled[k], whi[...], wlo[...])
                 send(multiply, lambda: prod_out, lambda: prod_in.at[k], PROD_S, PROD_R + k, (dp, c, c))
 
-        @pl.when(solver)
-        def _():
-            give_core0(solver, pulled, k, PF_S, P_R)
+        passes = mine if k == 0 else solver
+
+        @pl.when(passes)
+        def _():
+            give_core0(passes, pulled, k, PF_S, P_R)
 
         if k == 3:
 
@@ -557,7 +562,7 @@
                 arrived(back_in.at[at], BACK_R + at)
                 t = t - back_in[at]
             img[k] = upper(t, dhi.at[k - 2], dlo.at[k - 2], order)
-            spread(HIGH, k, at_high, img, IMG_S + 15 * (k - 2), IMG_R, [])
+            spread(HIGH, k, at_high, img, IMG_S + 15 * (k - 2), IMG_R, [], both=k == 3)
 
     for k in range(4):
         known = at_low | (solver & (c == k) & (r >= 2)) if k < 2 else at_high
@@ -566,9 +571,11 @@
         def _():
             arrived(img.at[k], IMG_R + k)
 
-        @pl.when(solver)
-        def _():
-            give_core0(solver, img, k, IMGF_S, IMG_R)
+        passes = at_high if k == 3 else solver
+
+        @pl.when(passes)
+        def _():
+            give_core0(passes, img, k, IMGF_S, IMG_R)
 
     load_res.wait()
     gamma = jnp.sum(rev[...] * rev[...], axis=1, keepdims=True)

time: 68.9 us -> 70.6 us (1.025)
  Pallas kernels: 66.2 us -> 67.7 us
    pallas_call x1, Pallas kernels: 66.2 us -> 67.7 us  [per_device(): pl.pallas_call(functools.partial(kernel, planes, total_rows), out_shape=(...]
where the time goes in v8:
time: 70.6 us; the launch traced here: 70.2 us
  Pallas kernels  67.7 us (96%)
  other arithmetic  1.86 us (3%)
    pallas_call x1, Pallas kernels, per_device(): pl.pallas_call(functools.partial(kernel, planes, total_rows), out_shape=(...  67.7 us
    add x1, other arithmetic, per_device(): new_direction = new_residual + betas * direction  1.86 us

profile of v8, /device:TPU:1, one launch (start us, length us, event | category | flops | bytes accessed | tf_op | source)
XLA Modules:
  0.0 70.2 jit_solution(9546759266270892428)
XLA Ops:
  0.6 67.7 %shard_map.103 = (f32[8,3072]{1,0:T(8,128)}, f32[8,3072]{1,0:T(8,128)}, f32[8,3072]{1,0:T(8,128)}) custom-call(f32[16,2048]{1,0:T(8,128)} %data.1, f32[16,768]{1,0:T(8,128)} %centres.1, f32[16]{0:T(128)} %scales.1, f32[768,768]{1,0:T(8,128)} %factor.1, f32[3,256,256]{2,1,0:T(8,128)} %block_inv.1, f32[8,3072]{1,0:T(8,128)} %residual.1, f32[8,3072]{1,0:T(8,128)} %direction.1), custom_call_target="tpu_custom_call" | custom-call | tf_op jit(solution)/shard_map/pallas_call | solution.py:609
  68.3 1.9 %multiply_add_fusion = (f32[8,3072]{1,0:T(8,128)}, f32[8,3072]{1,0:T(8,128)}, f32[8,3072]{1,0:T(8,128)}) fusion(f32[8,3072]{1,0:T(8,128)} %get-tuple-element.8, f32[8,3072]{1,0:T(8,128)} %direction.1, f32[8,3072]{1,0:T(8,128)} %residual.1, f32[8,3072]{1,0:T(8,128)} %get-tuple-element.6, f32[8,3072]{1,0:T(8,128)} %get-tuple-element.7, f32[8,3072]{1,0:T(8,128)} %param.13), kind=kLoop, calls=%fused_computation | loop fusion | flops 147456 | bytes 884736 | tf_op jit(solution)/shard_map/add | solution.py:651

commit v9 on v7

--- a/solution.py
+++ b/solution.py
@@ -388,6 +388,9 @@
             q = jnp.where(chip == 4 * a + b, k, q)
         return q
 
+    homes = [place_of(lax.rem(r + a, 4), lax.rem(c + b, 4)) for a, b in offsets]
+    place_here = homes[15]
+
     for k in (3, 2, 1, 0):
         mine = holders[k]
         nearby = [(k, j) for j in range(k - 1, -1, -1)]
@@ -434,7 +437,7 @@
     for i, (a, b) in enumerate(offsets):
         x = lax.rem(r + a, 4)
         y = lax.rem(c + b, 4)
-        chunk = place_of(x, y)
+        chunk = homes[i]
         owned = chunk < 12
         slot = 2 * i + core
 
@@ -462,7 +465,6 @@
             def _():
                 send(away, lambda chunk=chunk: nsend.at[chunk], lambda: nred.at[30], N_S + i, N_R, (2 * z + 1, x, y))
 
-    place_here = place_of(r, c)
     owner = solver & (place_here < 12)
 
     @pl.when(solver)
@@ -559,24 +561,28 @@
             img[k] = upper(t, dhi.at[k - 2], dlo.at[k - 2], order)
             spread(HIGH, k, at_high, img, IMG_S + 15 * (k - 2), IMG_R, [])
 
-    for k in range(4):
-        known = at_low | (solver & (c == k) & (r >= 2)) if k < 2 else at_high
-
-        @pl.when(jnp.logical_not(known))
-        def _():
-            arrived(img.at[k], IMG_R + k)
-
-        @pl.when(solver)
-        def _():
-            give_core0(solver, img, k, IMGF_S, IMG_R)
-
-    load_res.wait()
-    gamma = jnp.sum(rev[...] * rev[...], axis=1, keepdims=True)
     segs = [slice(k * width, (k + 1) * width) for k in range(4)]
     curvature = jnp.zeros((rhs, 1), f32)
     for k in range(4):
-        image[:, segs[k]] = img[k]
-        curvature += jnp.sum(div[:, segs[k]] * img[k], axis=1, keepdims=True)
+        if k == 3:
+            load_res.wait()
+            gamma = jnp.sum(rev[...] * rev[...], axis=1, keepdims=True)
+            for j in range(3):
+                image[:, segs[j]] = img[j]
+                curvature += jnp.sum(div[:, segs[j]] * img[j], axis=1, keepdims=True)
+            flush()
+        known = at_low | (solver & (c == k) & (r >= 2)) if k < 2 else at_high
+
+        @pl.when(jnp.logical_not(known))
+        def _():
+            arrived(img.at[k], IMG_R + k)
+
+        @pl.when(solver)
+        def _():
+            give_core0(solver, img, k, IMGF_S, IMG_R)
+
+    image[:, segs[3]] = img[3]
+    curvature += jnp.sum(div[:, segs[3]] * img[3], axis=1, keepdims=True)
     alpha = gamma / curvature
     gamma_next = jnp.zeros((rhs, 1), f32)
     for k in range(4):

time: 68.9 us -> 68.9 us (level)
  no operation moved by 1% of the time
where the time goes in v9:
time: 68.9 us; the launch traced here: 68.7 us
  Pallas kernels  66.2 us (96%)
  other arithmetic  1.86 us (3%)
    pallas_call x1, Pallas kernels, per_device(): pl.pallas_call(functools.partial(kernel, planes, total_rows), out_shape=(...  66.2 us
    add x1, other arithmetic, per_device(): new_direction = new_residual + betas * direction  1.86 us

profile of v9, /device:TPU:1, one launch (start us, length us, event | category | flops | bytes accessed | tf_op | source)
XLA Modules:
  0.0 68.7 jit_solution(339827157169068645)
XLA Ops:
  0.6 66.2 %shard_map.103 = (f32[8,3072]{1,0:T(8,128)}, f32[8,3072]{1,0:T(8,128)}, f32[8,3072]{1,0:T(8,128)}) custom-call(f32[16,2048]{1,0:T(8,128)} %data.1, f32[16,768]{1,0:T(8,128)} %centres.1, f32[16]{0:T(128)} %scales.1, f32[768,768]{1,0:T(8,128)} %factor.1, f32[3,256,256]{2,1,0:T(8,128)} %block_inv.1, f32[8,3072]{1,0:T(8,128)} %residual.1, f32[8,3072]{1,0:T(8,128)} %direction.1), custom_call_target="tpu_custom_call" | custom-call | tf_op jit(solution)/shard_map/pallas_call | solution.py:608
  66.8 1.9 %multiply_add_fusion = (f32[8,3072]{1,0:T(8,128)}, f32[8,3072]{1,0:T(8,128)}, f32[8,3072]{1,0:T(8,128)}) fusion(f32[8,3072]{1,0:T(8,128)} %get-tuple-element.8, f32[8,3072]{1,0:T(8,128)} %direction.1, f32[8,3072]{1,0:T(8,128)} %residual.1, f32[8,3072]{1,0:T(8,128)} %get-tuple-element.6, f32[8,3072]{1,0:T(8,128)} %get-tuple-element.7, f32[8,3072]{1,0:T(8,128)} %param.13), kind=kLoop, calls=%fused_computation | loop fusion | flops 147456 | bytes 884736 | tf_op jit(solution)/shard_map/add | solution.py:650

commit v10 on v9

--- a/solution.py
+++ b/solution.py
@@ -559,6 +559,7 @@
                 arrived(back_in.at[at], BACK_R + at)
                 t = t - back_in[at]
             img[k] = upper(t, dhi.at[k - 2], dlo.at[k - 2], order)
+        for k in (3, 2):
             spread(HIGH, k, at_high, img, IMG_S + 15 * (k - 2), IMG_R, [])
 
     segs = [slice(k * width, (k + 1) * width) for k in range(4)]

time: 68.9 us -> 70.6 us (1.025)
  Pallas kernels: 66.2 us -> 67.9 us
    pallas_call x1, Pallas kernels: 66.2 us -> 67.9 us  [per_device(): pl.pallas_call(functools.partial(kernel, planes, total_rows), out_shape=(...]
where the time goes in v10:
time: 70.6 us; the launch traced here: 70.4 us
  Pallas kernels  67.9 us (96%)
  other arithmetic  1.86 us (3%)
    pallas_call x1, Pallas kernels, per_device(): pl.pallas_call(functools.partial(kernel, planes, total_rows), out_shape=(...  67.9 us
    add x1, other arithmetic, per_device(): new_direction = new_residual + betas * direction  1.86 us

profile of v10, /device:TPU:1, one launch (start us, length us, event | category | flops | bytes accessed | tf_op | source)
XLA Modules:
  0.0 70.4 jit_solution(14565338593412631820)
XLA Ops:
  0.6 67.9 %shard_map.103 = (f32[8,3072]{1,0:T(8,128)}, f32[8,3072]{1,0:T(8,128)}, f32[8,3072]{1,0:T(8,128)}) custom-call(f32[16,2048]{1,0:T(8,128)} %data.1, f32[16,768]{1,0:T(8,128)} %centres.1, f32[16]{0:T(128)} %scales.1, f32[768,768]{1,0:T(8,128)} %factor.1, f32[3,256,256]{2,1,0:T(8,128)} %block_inv.1, f32[8,3072]{1,0:T(8,128)} %residual.1, f32[8,3072]{1,0:T(8,128)} %direction.1), custom_call_target="tpu_custom_call" | custom-call | tf_op jit(solution)/shard_map/pallas_call | solution.py:609
  68.5 1.9 %multiply_add_fusion = (f32[8,3072]{1,0:T(8,128)}, f32[8,3072]{1,0:T(8,128)}, f32[8,3072]{1,0:T(8,128)}) fusion(f32[8,3072]{1,0:T(8,128)} %get-tuple-element.8, f32[8,3072]{1,0:T(8,128)} %direction.1, f32[8,3072]{1,0:T(8,128)} %residual.1, f32[8,3072]{1,0:T(8,128)} %get-tuple-element.6, f32[8,3072]{1,0:T(8,128)} %get-tuple-element.7, f32[8,3072]{1,0:T(8,128)} %param.13), kind=kLoop, calls=%fused_computation | loop fusion | flops 147456 | bytes 884736 | tf_op jit(solution)/shard_map/add | solution.py:651
